TPU v7x, 32 devices: a whole 2x2x4 slice. The times are simulated.
32 devices in a mesh: dp: 16 (over z, x, core), tensor: 2 (over y).
Axes of the slice: x: 2, y: 2, z: 4, core: 2. Of those that a mesh axis runs over, the one named last changes fastest.
Arguments:
- tokens: bfloat16 [49152, 1024], P(('dp', 'tensor')), may hold values from -6 to 6
- seq_lengths: int32 [16, 3], P('dp'), may hold values from 0 to 1024, as said below
- first_gain: float32 [1024], replicated, may hold values from 0.5 to 1.5
- mix_weight: bfloat16 [1024, 6144], P(None, 'tensor'), may hold values from -0.1875 to 0.1875
- rate_weight: bfloat16 [1024, 16], P(None, 'tensor'), may hold values from -0.1875 to 0.1875
- conv_weight: float32 [4, 4096], P(None, 'tensor'), may hold values from -3 to 3
- decay_log: float32 [8], P('tensor'), may hold values from -4 to 1
- decay_bias: float32 [8], P('tensor'), may hold values from -4 to 1
- out_gain: float32 [256], replicated, may hold values from 0.5 to 1.5
- out_weight: bfloat16 [2048, 1024], P('tensor'), may hold values from -0.375 to 0.375
- second_gain: float32 [1024], replicated, may hold values from 0.5 to 1.5
- gate_weight: bfloat16 [1024, 2816], P(None, 'tensor'), may hold values from -0.1875 to 0.1875
- up_weight: bfloat16 [1024, 2816], P(None, 'tensor'), may hold values from -0.1875 to 0.1875
- down_weight: bfloat16 [2816, 1024], P('tensor'), may hold values from -0.109375 to 0.109375
- cotangent: bfloat16 [49152, 1024], P(('dp', 'tensor')), may hold values from -6 to 6
Outputs:
- block_out: bfloat16 [49152, 1024], P(('dp', 'tensor'))
- tokens_grad: bfloat16 [49152, 1024], P(('dp', 'tensor'))
- grad_first_gain: float32 [1024], replicated
- grad_mix_weight: float32 [1024, 6144], P(None, 'tensor')
- grad_rate_weight: float32 [1024, 16], P(None, 'tensor')
- grad_conv_weight: float32 [4, 4096], P(None, 'tensor')
- grad_decay_log: float32 [8], P('tensor')
- grad_decay_bias: float32 [8], P('tensor')
- grad_out_gain: float32 [256], replicated
- grad_out_weight: float32 [2048, 1024], P('tensor')
- grad_second_gain: float32 [1024], replicated
- grad_gate_weight: float32 [1024, 2816], P(None, 'tensor')
- grad_up_weight: float32 [1024, 2816], P(None, 'tensor')
- grad_down_weight: float32 [2816, 1024], P('tensor')
Inputs may be any that keep to these rules, and one draw needn't show every extreme that they name: `seq_lengths`: row g lists the lengths of the sequences packed in order from the first of group g's 3072 slots; its nonzero entries come first, two or more of them, each from 256 to 1024, and the rest are 0. In every draw one row holds 3 sequences of 1024 tokens and fills its group.
All inputs are finite; a program needn't handle non-finite values.
Results may differ from a plain program's by a relative error of at most 0.019.
Values may be sent and summed in bfloat16 or wider, within the bound.
No kernel may reach another device: no remote copies, remote signals or barrier semaphores. Data moves between devices by JAX's collectives and lax.ppermute only.
A program may use at most 640 MiB of HBM per device.

v0:
```python
from functools import partial

import jax
import jax.numpy as jnp
from jax import lax
from jax.sharding import PartitionSpec as P

DK = 128
DV = 256
CONV = 4
SPAN = 64


HIGH = lax.Precision.HIGHEST


def rms_norm(value, gain):
    return value * lax.rsqrt(jnp.mean(value * value, axis=-1, keepdims=True) + 1e-05) * gain


def layout(lengths, capacity):
    bounds = jnp.cumsum(lengths)
    position = jnp.arange(capacity, dtype=jnp.int32)
    segment = jnp.sum((position[:, None] >= bounds[None, :]).astype(jnp.int32), axis=1)
    live = (position < bounds[-1]).astype(jnp.float32)[:, None]
    return (segment, live)


def delta_head(query, keys, values, beta, decay, segment, span):
    total = query.shape[0]
    blocks = total // span
    q_block = query.reshape(blocks, span, -1)
    k_block = keys.reshape(blocks, span, -1)
    v_block = values.reshape(blocks, span, -1)
    b_block = beta.reshape(blocks, span)
    cumulative = jnp.cumsum(decay.reshape(blocks, span), axis=1)
    s_block = segment.reshape(blocks, span)
    before = jnp.concatenate([jnp.full((1,), -1, jnp.int32), s_block[:-1, -1]])
    carried = (s_block == before[:, None]).astype(jnp.float32)
    order = jnp.arange(span)
    within = (order[:, None] >= order[None, :])[None] & (s_block[:, :, None] == s_block[:, None, :])
    strict = within & (order[:, None] > order[None, :])[None]
    spread = jnp.where(within, cumulative[:, :, None] - cumulative[:, None, :], 0.0)
    fading = jnp.where(within, jnp.exp(spread), 0.0)
    inner = jnp.einsum("nid,njd->nij", k_block, k_block, precision=HIGH)
    lower = jnp.where(strict, b_block[:, :, None] * inner * fading, 0.0)
    system = jnp.eye(span, dtype=jnp.float32)[None] + lower
    start = jnp.exp(cumulative) * carried
    right = jnp.concatenate(
        [b_block[:, :, None] * v_block, (b_block * start)[:, :, None] * k_block], axis=-1
    )
    solved = lax.linalg.triangular_solve(
        system, right, left_side=True, lower=True, unit_diagonal=True
    )
    width = v_block.shape[-1]
    u_part = solved[..., :width]
    w_part = solved[..., width:]
    scores = jnp.einsum("nid,njd->nij", q_block, k_block, precision=HIGH) * fading
    q_start = q_block * start[:, :, None]
    k_end = k_block * fading[:, -1, :, None]
    factor = start[:, -1]

    def step(state, pieces):
        w_now, u_now, k_now, q_now, s_now, f_now = pieces
        fresh = u_now - jnp.dot(w_now, state, precision=HIGH)
        out_now = jnp.dot(q_now, state, precision=HIGH) + jnp.dot(s_now, fresh, precision=HIGH)
        grown = f_now * state + lax.dot_general(
            k_now, fresh, (((0,), (0,)), ((), ())), precision=HIGH
        )
        return (grown, out_now)

    initial = jnp.zeros((k_block.shape[-1], width), jnp.float32)
    final, outputs = lax.scan(
        jax.checkpoint(step), initial, (w_part, u_part, k_end, q_start, scores, factor)
    )
    return outputs.reshape(total, width)


def mixer(proj, rates, conv_w, decay_log, decay_bias, out_gain, segment, span):
    total = proj.shape[0]
    heads = decay_log.shape[0]
    lanes = 2 * DK + DV
    pieces = proj.reshape(total, heads, lanes + DV)
    blended = pieces[..., :lanes]
    gate_out = pieces[..., lanes:]
    taps = conv_w.reshape(CONV, heads, lanes)
    summed = jnp.zeros_like(blended)
    for back in range(CONV):
        moved = jnp.pad(blended, ((back, 0), (0, 0), (0, 0)))[:total]
        prior = jnp.pad(segment, (back, 0), constant_values=-1)[:total]
        summed = (
            summed
            + jnp.where((prior == segment)[:, None, None], moved, 0.0) * taps[CONV - 1 - back]
        )
    activated = jax.nn.silu(summed)
    query = activated[..., :DK]
    keys = activated[..., DK : 2 * DK]
    values = activated[..., 2 * DK :]
    query = query * lax.rsqrt(jnp.sum(query * query, axis=-1, keepdims=True) + 1e-06) * DK ** (-0.5)
    keys = keys * lax.rsqrt(jnp.sum(keys * keys, axis=-1, keepdims=True) + 1e-06)
    halves = rates.reshape(total, heads, 2)
    beta = jax.nn.sigmoid(halves[..., 0])
    decay = -jnp.exp(decay_log) * jax.nn.softplus(halves[..., 1] + decay_bias)
    delta_out = jax.vmap(partial(delta_head, span=span), in_axes=(1, 1, 1, 1, 1, None), out_axes=1)(
        query, keys, values, beta, decay, segment
    )
    scaled = (
        delta_out
        * lax.rsqrt(jnp.mean(delta_out * delta_out, axis=-1, keepdims=True) + 1e-05)
        * out_gain
    )
    return (scaled * jax.nn.silu(gate_out)).reshape(total, heads * DV)


def cross(left, right):
    return lax.dot_general(
        left, right, (((0,), (0,)), ((), ())), preferred_element_type=jnp.float32
    )


def back_dot(grad, weight):
    return lax.dot_general(
        grad, weight, (((1,), (1,)), ((), ())), preferred_element_type=jnp.float32
    )


def on_device(
    tokens,
    seq_lengths,
    first_gain,
    mix_weight,
    rate_weight,
    conv_weight,
    decay_log,
    decay_bias,
    out_gain,
    out_weight,
    second_gain,
    gate_weight,
    up_weight,
    down_weight,
    cotangent,
):
    rows = tokens.shape[0]
    members = lax.axis_size("tensor")
    capacity = rows * members
    here = lax.axis_index("tensor")
    segment, live_all = layout(seq_lengths[0], capacity)
    live = lax.dynamic_slice_in_dim(live_all, here * rows, rows, 0)
    inputs = tokens.astype(jnp.float32)
    first_normed, first_back = jax.vjp(rms_norm, inputs, first_gain)
    first_low = first_normed.astype(jnp.bfloat16)
    first_rows = lax.all_gather(first_low, "tensor", axis=0, tiled=True)
    proj = jnp.dot(first_rows, mix_weight, preferred_element_type=jnp.float32)
    rates = jnp.dot(first_rows, rate_weight, preferred_element_type=jnp.float32)

    def local_mixer(proj_in, rates_in, taps_in, log_in, bias_in, gain_in):
        return mixer(proj_in, rates_in, taps_in, log_in, bias_in, gain_in, segment, SPAN)

    mixed, mixer_back = jax.vjp(
        local_mixer, proj, rates, conv_weight, decay_log, decay_bias, out_gain
    )
    mixed_low = mixed.astype(jnp.bfloat16)
    attn = lax.psum_scatter(
        jnp.dot(mixed_low, out_weight, preferred_element_type=jnp.float32),
        "tensor",
        scatter_dimension=0,
        tiled=True,
    )
    residual = inputs + live * attn
    second_normed, second_back = jax.vjp(rms_norm, residual, second_gain)
    second_low = second_normed.astype(jnp.bfloat16)
    second_rows = lax.all_gather(second_low, "tensor", axis=0, tiled=True)
    gate = jnp.dot(second_rows, gate_weight, preferred_element_type=jnp.float32)
    up = jnp.dot(second_rows, up_weight, preferred_element_type=jnp.float32)
    sigma = jax.nn.sigmoid(gate)
    gated = gate * sigma
    hidden = (gated * up).astype(jnp.bfloat16)
    ffn = lax.psum_scatter(
        jnp.dot(hidden, down_weight, preferred_element_type=jnp.float32).astype(jnp.bfloat16),
        "tensor",
        scatter_dimension=0,
        tiled=True,
    ).astype(jnp.float32)
    block_out = (residual + live * ffn).astype(jnp.bfloat16)
    out_grad = cotangent.astype(jnp.float32)
    ffn_grad = lax.all_gather((live * out_grad).astype(jnp.bfloat16), "tensor", axis=0, tiled=True)
    grad_down = cross(hidden, ffn_grad)
    hidden_grad = back_dot(ffn_grad, down_weight)
    gate_grad = (hidden_grad * up * (sigma * (1.0 + gate * (1.0 - sigma)))).astype(jnp.bfloat16)
    up_grad = (hidden_grad * gated).astype(jnp.bfloat16)
    grad_gate = cross(second_rows, gate_grad)
    grad_up = cross(second_rows, up_grad)
    second_sum = lax.psum_scatter(
        (back_dot(gate_grad, gate_weight) + back_dot(up_grad, up_weight)).astype(jnp.bfloat16),
        "tensor",
        scatter_dimension=0,
        tiled=True,
    ).astype(jnp.float32)
    residual_part, second_gain_part = second_back(second_sum)
    residual_grad = out_grad + residual_part
    attn_grad = lax.all_gather(
        (live * residual_grad).astype(jnp.bfloat16), "tensor", axis=0, tiled=True
    )
    grad_out = cross(mixed_low, attn_grad)
    mixed_grad = back_dot(attn_grad, out_weight)
    proj_grad, rates_grad, grad_conv, grad_log, grad_bias, out_gain_part = mixer_back(mixed_grad)
    proj_low = proj_grad.astype(jnp.bfloat16)
    rates_low = rates_grad.astype(jnp.bfloat16)
    grad_mix = cross(first_rows, proj_low)
    grad_rate = cross(first_rows, rates_low)
    first_sum = lax.psum_scatter(
        (back_dot(proj_low, mix_weight) + back_dot(rates_low, rate_weight)).astype(jnp.bfloat16),
        "tensor",
        scatter_dimension=0,
        tiled=True,
    ).astype(jnp.float32)
    input_part, first_gain_part = first_back(first_sum)
    tokens_grad = (residual_grad + input_part).astype(jnp.bfloat16)
    grad_first, grad_outg, grad_second = lax.psum(
        (first_gain_part, out_gain_part, second_gain_part), ("dp", "tensor")
    )
    grad_mix, grad_rate, grad_conv, grad_log, grad_bias, grad_out, grad_gate, grad_up, grad_down = (
        lax.psum(grad_mix.astype(jnp.bfloat16), "dp").astype(jnp.float32),
        lax.psum(grad_rate.astype(jnp.bfloat16), "dp").astype(jnp.float32),
        lax.psum(grad_conv.astype(jnp.bfloat16), "dp").astype(jnp.float32),
        lax.psum(grad_log.astype(jnp.bfloat16), "dp").astype(jnp.float32),
        lax.psum(grad_bias.astype(jnp.bfloat16), "dp").astype(jnp.float32),
        lax.psum(grad_out.astype(jnp.bfloat16), "dp").astype(jnp.float32),
        lax.psum(grad_gate.astype(jnp.bfloat16), "dp").astype(jnp.float32),
        lax.psum(grad_up.astype(jnp.bfloat16), "dp").astype(jnp.float32),
        lax.psum(grad_down.astype(jnp.bfloat16), "dp").astype(jnp.float32),
    )
    return (
        block_out,
        tokens_grad,
        grad_first,
        grad_mix,
        grad_rate,
        grad_conv,
        grad_log,
        grad_bias,
        grad_outg,
        grad_out,
        grad_second,
        grad_gate,
        grad_up,
        grad_down,
    )


def solution(mesh):
    placed = (
        P(("dp", "tensor"), None),
        P("dp", None),
        P(),
        P(None, "tensor"),
        P(None, "tensor"),
        P(None, "tensor"),
        P("tensor"),
        P("tensor"),
        P(),
        P("tensor", None),
        P(),
        P(None, "tensor"),
        P(None, "tensor"),
        P("tensor", None),
        P(("dp", "tensor"), None),
    )
    return jax.shard_map(
        on_device,
        mesh=mesh,
        in_specs=placed,
        out_specs=(
            P(("dp", "tensor"), None),
            P(("dp", "tensor"), None),
            P(),
            P(None, "tensor"),
            P(None, "tensor"),
            P(None, "tensor"),
            P("tensor"),
            P("tensor"),
            P(),
            P("tensor", None),
            P(),
            P(None, "tensor"),
            P(None, "tensor"),
            P("tensor", None),
        ),
        check_vma=False,
    )
```

profile of v0, /device:TPU:0, one launch (start us, length us, event | category | flops | bytes accessed | tf_op | source)
XLA Modules:
  0.0 3401.9 jit_solution(479901195134551166)
XLA Ops:
  25.0 73.8 %all-gather.5.cloned.1.call-done = bf16[3072,1024]{1,0:T(8,128)(2,1)} async-done(((bf16[1536,1024]{1,0:T(8,128)(2,1)}), bf16[3072,1024]{1,0:T(8,128)(2,1)}) %all-gather.5.cloned.1.call-update) | async-done | bytes 6291472 | tf_op jit(solution)/shard_map/all_gather | solution.py:153
  98.8 27.5 fusion.117
  137.0 17.8 slice.115
  154.7 24.7 copy.392
  179.5 48.8 %fusion.39 = (f32[3072,4,512]{2,0,1:T(8,128)}, f32[3072,4,512]{2,0,1:T(8,128)}) fusion(f32[4,512]{1,0:T(4,128)S(1)} %mul.661, f32[3072,4,512]{2,0,1:T(8,128)} %copy.392, pred[3072]{0:T(1024)(128)(4,1)S(1)} %get-tuple-element.809, f32[4,512]{1,0:T(4,128)S(1)} %mul.658, pred[3072]{0:T(1024)(128)(4,1)S(1)} %get-tuple-element.808, f32[4,512]{1,0:T(4,128)S(1)} %mul.655, ...), kind=kLoop, calls=%fused_computation.79 | loop fusion | flops 88080384 | bytes 75539456 | tf_op jit(solution)/shard_map/jvp(jit(silu))/mul | solution.py:95
  316.3 265.1 %custom-call.7 = f32[4,48,1,64,64]{1,3,4,2,0:T(8,128)} custom-call(f32[4,48,1,64,64]{1,4,3,2,0:T(8,128)} %get-tuple-element.796), custom_call_target="InvertDiagBlocksLowerTriangular" | custom-call | tf_op jit(solution)/shard_map/jvp(vmap())/triangular_solve | solution.py:52
  600.6 21.6 fusion.40
  640.5 12.6 copy.394
  682.4 16.3 bitcast_multiply_fusion.14
  698.7 350.3 %while.42 = (s32[]{:T(128)}, f32[4,128,256]{2,1,0:T(8,128)S(1)}, f32[48,4,64,256]{3,2,0,1:T(8,128)}, f32[48,4,128,256]{3,2,1,0:T(8,128)}, f32[48,4]{1,0:T(8,128)...) while((s32[]{:T(128)}, f32[4,128,256]{2,1,0:T(8,128)S(1)}, ...), condition=%wide.region_7.8_spmd.clone, body=%wide.region_6.7_spmd.clone.sunk | while | flops 353239040 | bytes 5507785 | solution.py:73
  1056.6 12.6 multiply_convert_fusion.3
  1091.9 142.7 %reduce-scatter.5.cloned.1.call-done = f32[1536,1024]{1,0:T(8,128)} async-done(((f32[3072,1024]{1,0:T(8,128)}), f32[1536,1024]{1,0:T(8,128)}) %reduce-scatter.5.cloned.1.call-update) | async-done | bytes 6291472 | tf_op jit(solution)/shard_map/reduce_scatter | solution.py:164
  1246.9 79.9 %all-gather.7.cloned.1.call-done = bf16[3072,1024]{1,0:T(8,128)(2,1)} async-done(((bf16[1536,1024]{1,0:T(8,128)(2,1)}), bf16[3072,1024]{1,0:T(8,128)(2,1)}) %all-gather.7.cloned.1.call-update) | async-done | bytes 6291472 | tf_op jit(solution)/shard_map/all_gather | solution.py:173
  1326.8 17.2 fusion.121
  1344.0 12.7 fusion.120
  1356.7 52.5 %all-gather.9.cloned.1.call-done = bf16[3072,1024]{1,0:T(8,128)(2,1)} async-done(((bf16[1536,1024]{1,0:T(8,128)(2,1)}), bf16[3072,1024]{1,0:T(8,128)(2,1)}) %all-gather.9.cloned.1.call-update) | async-done | bytes 6291472 | tf_op jit(solution)/shard_map/all_gather | solution.py:187
  1409.2 29.7 multiply_convert_fusion
  1438.9 16.4 fusion.122
  1455.3 16.4 add_convert_fusion.2
  1471.7 14.1 convolution_convert_fusion.1
  1485.9 63.0 %reduce-scatter.9.cloned.1.call-done = bf16[1536,1024]{1,0:T(8,128)(2,1)} async-done(((bf16[3072,1024]{1,0:T(8,128)(2,1)}), bf16[1536,1024]{1,0:T(8,128)(2,1)}) %reduce-scatter.9.cloned.1.call-update) | async-done | bytes 3145744 | tf_op jit(solution)/shard_map/reduce_scatter | solution.py:194
  1554.4 73.8 %reduce-scatter.7.cloned.1.call-done = bf16[1536,1024]{1,0:T(8,128)(2,1)} async-done(((bf16[3072,1024]{1,0:T(8,128)(2,1)}), bf16[1536,1024]{1,0:T(8,128)(2,1)}) %reduce-scatter.7.cloned.1.call-update) | async-done | bytes 3145744 | tf_op jit(solution)/shard_map/reduce_scatter | solution.py:179
  1654.6 15.8 convolution_convert_fusion.3
  1670.4 15.7 convolution_convert_fusion.4
  1686.1 13.1 convolution_convert_fusion.2
  1699.2 18.2 all-gather.11.cloned.1.call-done
  1729.8 12.6 copy.346
  1742.4 19.7 multiply_reduce_fusion.5
  1762.4 13.8 add_add_fusion
  1796.5 725.8 %while.43 = (s32[]{:T(128)}, f32[4,128,256]{2,1,0:T(8,128)S(1)}, f32[48,4,64,128]{3,2,1,0:T(8,128)}, f32[48,4,64,256]{3,2,1,0:T(8,128)}, f32[48,4,64,128]{3,2,0,...) while((s32[]{:T(128)}, f32[4,128,256]{2,1,0:T(8,128)S(1)}, ...), condition=%wide.region_17.18_spmd.clone, body=%wide.region_15.17_spmd.clone.sunk | while | flops 806354944 | bytes 14745951 | solution.py:73
  2522.3 26.2 fusion.44
  2574.5 23.9 fusion.46
  2598.4 15.3 slice_multiply_fusion
  2622.9 21.9 fusion.59
  2661.6 14.8 fusion.124
  2688.5 14.0 fusion.126
  2702.5 18.1 fusion.83
  2743.0 58.8 %multiply_reduce_fusion.4 = (f32[4,512]{1,0:T(4,128)}, f32[4,512]{1,0:T(4,128)}, f32[4,512]{1,0:T(4,128)}, f32[4,512]{1,0:T(4,128)}, f32[3072,4,512]{2,0,1:T(8,128)}) fusion(f32[3072,4,512]{2,0,1:T(8,128)} %copy.392, pred[3072]{0:T(1024)(128)(4,1)S(1)} %copy-done.86, pred[3072]{0:T(1024)(128)(4,1)S(1)} %copy-done.88, pred[3072]{0:T(1024)(128)(4,1)S(1)} %copy-done.84, ...), kind=kLoop, calls=%fused_computation.74 | loop fusion | flops 138403840 | bytes 100705280 | tf_op jit(solution)/shard_map/transpose(jvp())/reduce_sum | solution.py:93
  2801.8 32.6 multiply_select_fusion
  2834.4 41.5 %fusion.36 = f32[3072,4,512]{2,0,1:T(8,128)} fusion(f32[3072,4,512]{2,0,1:T(8,128)} %get-tuple-element.781, f32[3072,4,512]{2,0,1:T(8,128)} %get-tuple-element.780, f32[3072,4,512]{2,0,1:T(8,128)} %get-tuple-element.779, f32[3072,4,512]{2,0,1:T(8,128)} %get-tuple-element.764, f32[4,512]{1,0:T(4,128)S(1)} %copy-done.66), kind=kLoop, calls=%fused_computation.68 | loop fusion | flops 25165824 | bytes 125837312 | tf_op jit(solution)/shard_map/transpose(jvp())/add_any | solution.py:89
  2875.9 19.7 add_convert_fusion
  2895.6 24.6 copy.369
  2931.9 24.3 convolution_convert_fusion
  2979.0 27.6 add_convert_fusion.1
  3011.2 65.3 %all-reduce.25 = (bf16[1024,8]{0,1:T(8,128)(2,1)S(1)}, bf16[4,2048]{1,0:T(4,128)(2,1)S(1)}, bf16[4]{0:T(256)(128)(2,1)S(1)}, bf16[4]{0:T(256)(128)(2,1)S(1)}) all-reduce(bf16[1024,8]{0,1:T(8,128)(2,1)S(1)} %convolution_convert_fusion.6, bf16[4,2048]{1,0:T(4,128)(2,1)S(1)} %bitcast.421, ...), channel_id=1, replica_groups=mesh['dp'=16,'tensor'=2] {'dp'}, use_global_device_ids=true, to_apply=%region_33.34 | all-reduce | flops 16392 | bytes 65568 | tf_op jit(solution)/shard_map/psum | solution.py:225
  3078.8 183.1 %all-reduce.29.cloned.1.call-done = (bf16[1024,3072]{1,0:T(8,128)(2,1)}, bf16[1024,1024]{1,0:T(8,128)(2,1)}, bf16[1024,1408]{1,0:T(8,128)(2,1)}, bf16[1024,1408]{1,0:T(8,128)(2,1)}, bf16[1408,1024]{1,0:T(8,128)(2,1)}) async-done(((bf16[1024,3072]{1,0:T(8,128)(2,1)}, bf16[1024,1024]{1,0:T(8,128)(2,1)}, bf16[1024,1408]{1,0:T(8,128)(2,1)}, bf16[1024,1408]{1,0:T(8,128)(2,1)}, bf16[1408,1024]{1,0:T(8,128)(2,1)}), ...) | async-done | bytes 17039376 | tf_op jit(solution)/shard_map/psum | solution.py:224
  3283.0 58.1 %reduce-scatter.11.cloned.1.call-done = bf16[1536,1024]{1,0:T(8,128)(2,1)} async-done(((bf16[3072,1024]{1,0:T(8,128)(2,1)}), bf16[1536,1024]{1,0:T(8,128)(2,1)}) %reduce-scatter.11.cloned.1.call-update) | async-done | bytes 3145744 | tf_op jit(solution)/shard_map/reduce_scatter | solution.py:212
  3345.9 39.6 %all-reduce.24 = (f32[1024]{0:T(1024)}, f32[256]{0:T(256)}, f32[1024]{0:T(1024)}) all-reduce(f32[1024]{0:T(1024)S(1)} %get-tuple-element.690, f32[256]{0:T(256)S(1)} %copy-done.100, f32[1024]{0:T(1024)S(1)} %copy-done.97), channel_id=1, replica_groups=mesh['dp'=16,'tensor'=2] {'dp','tensor'}, use_global_device_ids=true, to_apply=%region_31.32 | all-reduce | flops 2304 | bytes 18432 | tf_op jit(solution)/shard_map/psum | solution.py:220
  (1641 shorter events, 1523.4 us)
Async XLA Ops:
  7.2 1402.0 %copy-start = (bf16[1408,1024]{1,0:T(8,128)(2,1)S(1)}, bf16[1408,1024]{1,0:T(8,128)(2,1)}, u32[]{:S(2)}) copy-start(bf16[1408,1024]{1,0:T(8,128)(2,1)} %param.32) | copy-start | bytes 8650756
  7.2 91.6 %all-gather.5.cloned.1.call-start = ((), (), s32[]{:S(2)}) async-start(), calls=%async_computation.4 | async-start | bytes 9437184 | tf_op jit(solution)/shard_map/all_gather | solution.py:153
  15.5 1219.1 %reduce-scatter.5.cloned.1.call-start = ((), (), s32[]{:S(2)}) async-start(), calls=%async_computation.5 | async-start | bytes 18874368 | tf_op jit(solution)/shard_map/reduce_scatter | solution.py:164
  16.7 162.8 %copy-start.65 = (f32[4,512]{1,0:T(4,128)}, f32[4,512]{1,0:T(4,128)S(1)}, u32[]{:S(2)}) copy-start(f32[4,512]{1,0:T(4,128)S(1)} %mul.652) | copy-start | bytes 24580
  16.7 162.7 %copy-start.67 = (f32[4,512]{1,0:T(4,128)}, f32[4,512]{1,0:T(4,128)S(1)}, u32[]{:S(2)}) copy-start(f32[4,512]{1,0:T(4,128)S(1)} %mul.655) | copy-start | bytes 24580
  16.8 162.7 %copy-start.69 = (f32[4,512]{1,0:T(4,128)}, f32[4,512]{1,0:T(4,128)S(1)}, u32[]{:S(2)}) copy-start(f32[4,512]{1,0:T(4,128)S(1)} %mul.661) | copy-start | bytes 24580
  16.8 162.7 %copy-start.71 = (f32[4,512]{1,0:T(4,128)}, f32[4,512]{1,0:T(4,128)S(1)}, u32[]{:S(2)}) copy-start(f32[4,512]{1,0:T(4,128)S(1)} %mul.658) | copy-start | bytes 24580
  19.2 288.6 %copy-start.13 = (pred[48,64,64]{0,2,1:T(8,128)(4,1)}, pred[48,64,64]{0,2,1:T(8,128)(4,1)S(1)}, u32[]{:S(2)}) copy-start(pred[48,64,64]{0,2,1:T(8,128)(4,1)S(1)} %get-tuple-element.806) | copy-start | bytes 589828
  24.3 155.2 %copy-start.83 = (pred[3072]{0:T(1024)(128)(4,1)}, pred[3072]{0:T(1024)(128)(4,1)S(1)}, u32[]{:S(2)}) copy-start(pred[3072]{0:T(1024)(128)(4,1)S(1)} %get-tuple-element.808) | copy-start | bytes 9220
  24.3 155.2 %copy-start.85 = (pred[3072]{0:T(1024)(128)(4,1)}, pred[3072]{0:T(1024)(128)(4,1)S(1)}, u32[]{:S(2)}) copy-start(pred[3072]{0:T(1024)(128)(4,1)S(1)} %get-tuple-element.809) | copy-start | bytes 9220
  24.3 155.2 %copy-start.87 = (pred[3072]{0:T(1024)(128)(4,1)}, pred[3072]{0:T(1024)(128)(4,1)S(1)}, u32[]{:S(2)}) copy-start(pred[3072]{0:T(1024)(128)(4,1)S(1)} %get-tuple-element.810) | copy-start | bytes 9220
  235.6 28.7 copy-start.44
  256.4 39.7 %copy-start.17 = (f32[4,48,64]{2,1,0:T(8,128)}, f32[4,48,64]{2,1,0:T(8,128)S(1)}, u32[]{:S(2)}) copy-start(f32[4,48,64]{2,1,0:T(8,128)S(1)} %mul.671) | copy-start | bytes 147460
  1090.0 236.8 %all-gather.7.cloned.1.call-start = ((), (), s32[]{:S(2)}) async-start(), calls=%async_computation.6 | async-start | bytes 9437184 | tf_op jit(solution)/shard_map/all_gather | solution.py:173
  1091.9 149.5 %copy-start.63 = (f32[1536]{0:T(1024)}, f32[1536]{0:T(1024)S(1)}, u32[]{:S(2)}) copy-start(f32[1536]{0:T(1024)S(1)} %fusion.104) | copy-start | bytes 18436
  1091.9 152.1 %copy-start.79 = (f32[1024]{0:T(1024)S(1)}, f32[1024]{0:T(1024)}, u32[]{:S(2)}) copy-start(f32[1024]{0:T(1024)} %param.29) | copy-start | bytes 12292
  1242.0 386.3 %copy-start.53 = (f32[1536]{0:T(1024)}, f32[1536]{0:T(1024)S(1)}, u32[]{:S(2)}) copy-start(f32[1536]{0:T(1024)S(1)} %fusion.106) | copy-start | bytes 18436
  1246.3 162.9 %all-gather.9.cloned.1.call-start = ((), (), s32[]{:S(2)}) async-start(), calls=%async_computation.8 | async-start | bytes 9437184 | tf_op jit(solution)/shard_map/all_gather | solution.py:187
  1246.8 302.1 %reduce-scatter.9.cloned.1.call-start = ((), (), s32[]{:S(2)}) async-start(), calls=%async_computation.9 | async-start | bytes 9437184 | tf_op jit(solution)/shard_map/reduce_scatter | solution.py:194
  1326.8 17.2 copy-start.105
  1326.8 17.2 copy-start.106
  1471.7 156.6 %reduce-scatter.7.cloned.1.call-start = ((), (), s32[]{:S(2)}) async-start(), calls=%async_computation.7 | async-start | bytes 9437184 | tf_op jit(solution)/shard_map/reduce_scatter | solution.py:179
  1485.8 68.6 %copy-start.76 = (f32[1536]{0:T(1024)S(1)}, f32[1536]{0:T(1024)}, u32[]{:S(2)}) copy-start(f32[1536]{0:T(1024)} %copy-done.75) | copy-start | bytes 18436
  1485.8 142.4 %copy-start.64 = (f32[1536]{0:T(1024)S(1)}, f32[1536]{0:T(1024)}, u32[]{:S(2)}) copy-start(f32[1536]{0:T(1024)} %copy-done.63) | copy-start | bytes 18436
  1485.9 231.6 %all-gather.11.cloned.1.call-start = ((), (), s32[]{:S(2)}) async-start(), calls=%async_computation.10 | async-start | bytes 9437184 | tf_op jit(solution)/shard_map/all_gather | solution.py:202
  1554.4 82.5 %copy-start.61 = (f32[1536]{0:T(1024)}, f32[1536]{0:T(1024)S(1)}, u32[]{:S(2)}) copy-start(f32[1536]{0:T(1024)S(1)} %multiply_multiply_fusion.5) | copy-start | bytes 18436
  1636.9 1624.9 %all-reduce.29.cloned.1.call-start = ((), (), s32[]{:S(2)}) async-start(), calls=%async_computation.12 | async-start | bytes 34078720 | tf_op jit(solution)/shard_map/psum | solution.py:224
  1654.5 31.5 slice-start.4
  1654.6 31.5 slice-start.5
  1686.1 31.4 copy-start.108
  1742.4 19.7 copy-start.43
  1742.4 20.0 copy-start.5
  2522.3 26.2 copy-start.59
  2574.5 23.9 copy-start.18
  2743.0 58.9 %copy-start.68 = (f32[4,512]{1,0:T(4,128)S(1)}, f32[4,512]{1,0:T(4,128)}, u32[]{:S(2)}) copy-start(f32[4,512]{1,0:T(4,128)} %copy-done.67) | copy-start | bytes 24580
  2743.0 58.8 %copy-start.70 = (f32[4,512]{1,0:T(4,128)S(1)}, f32[4,512]{1,0:T(4,128)}, u32[]{:S(2)}) copy-start(f32[4,512]{1,0:T(4,128)} %copy-done.69) | copy-start | bytes 24580
  2743.0 58.8 %copy-start.72 = (f32[4,512]{1,0:T(4,128)S(1)}, f32[4,512]{1,0:T(4,128)}, u32[]{:S(2)}) copy-start(f32[4,512]{1,0:T(4,128)} %copy-done.71) | copy-start | bytes 24580
  2801.8 32.6 copy-start.66
  2956.2 384.9 %reduce-scatter.11.cloned.1.call-start = ((), (), s32[]{:S(2)}) async-start(), calls=%async_computation.11 | async-start | bytes 9437184 | tf_op jit(solution)/shard_map/reduce_scatter | solution.py:212
  3276.5 64.6 %copy-start.56 = (f32[1536]{0:T(1024)S(1)}, f32[1536]{0:T(1024)}, u32[]{:S(2)}) copy-start(f32[1536]{0:T(1024)} %copy-done.55) | copy-start | bytes 18436
  3276.5 64.6 %copy-start.90 = (f32[1024]{0:T(1024)S(1)}, f32[1024]{0:T(1024)}, u32[]{:S(2)}) copy-start(f32[1024]{0:T(1024)} %param.21) | copy-start | bytes 12292
  3283.0 62.9 %copy-start.74 = (f32[1536]{0:T(1024)S(1)}, f32[1536]{0:T(1024)}, u32[]{:S(2)}) copy-start(f32[1536]{0:T(1024)} %copy-done.73) | copy-start | bytes 18436
  3283.0 62.9 %copy-start.97 = (f32[1024]{0:T(1024)S(1)}, f32[1024]{0:T(1024)}, u32[]{:S(2)}) copy-start(f32[1024]{0:T(1024)} %get-tuple-element.686) | copy-start | bytes 12292
  3283.0 62.9 %copy-start.100 = (f32[256]{0:T(256)S(1)}, f32[256]{0:T(256)}, u32[]{:S(2)}) copy-start(f32[256]{0:T(256)} %get-tuple-element.680) | copy-start | bytes 3076
  3283.0 102.5 %copy-start.54 = (f32[1536]{0:T(1024)S(1)}, f32[1536]{0:T(1024)}, u32[]{:S(2)}) copy-start(f32[1536]{0:T(1024)} %copy-done.53) | copy-start | bytes 18436
  3283.0 102.5 %copy-start.62 = (f32[1536]{0:T(1024)S(1)}, f32[1536]{0:T(1024)}, u32[]{:S(2)}) copy-start(f32[1536]{0:T(1024)} %copy-done.61) | copy-start | bytes 18436
  3283.0 102.5 %copy-start.80 = (f32[1024]{0:T(1024)S(1)}, f32[1024]{0:T(1024)}, u32[]{:S(2)}) copy-start(f32[1024]{0:T(1024)} %param.29) | copy-start | bytes 12292
  3345.9 49.1 %copy-start.1 = (bf16[1408,1024]{1,0:T(8,128)(2,1)S(1)}, bf16[1408,1024]{1,0:T(8,128)(2,1)}, u32[]{:S(2)}) copy-start(bf16[1408,1024]{1,0:T(8,128)(2,1)} %param.32) | copy-start | bytes 8650756
  (80 other events, 651.0 us)
Sparse Core Ops, SparseCore 0:
  15.7 83.0 all-gather.4
  1090.2 144.4 reduce-scatter.4
  1246.4 80.3 all-gather.6
  1328.8 80.3 all-gather.8
  1471.8 77.0 reduce-scatter.8
  1551.2 77.0 reduce-scatter.6
  1637.0 80.3 all-gather.10
  2956.3 305.5 all-reduce.28
  3264.2 76.9 reduce-scatter.10
where the time goes:
time: 3430 us; the launch traced here: 3400 us
  matrix products  1150 us (34%)
  other arithmetic  784 us (23%)
  waiting for transfers between devices  746 us (22%)
  local copies, waits for them, and re-layouts  597 us (17%)
  blocking collectives  105 us (3%)
    another operation x5, other arithmetic, delta_head(): lax.linalg.triangular_solve(system, right, left_side=True, lower=True, un...  275 us
    squeeze x288, local copies, waits for them, and re-layouts, delta_head(): lax.scan(jax.checkpoint(step), initial, (w_part, u_part, k_end, q_start,...  271 us
    dot_general x144, matrix products, step(): jnp.dot(s_now, fresh, precision=HIGH)  196 us
    dot_general x192, matrix products, step(): fresh = u_now - jnp.dot(w_now, state, precision=HIGH)  184 us
    psum x1, waiting for transfers between devices, on_device(): lax.psum(grad_mix.astype(jnp.bfloat16), 'dp').astype(jnp.float32)  183 us
    dot_general x144, matrix products, step(): lax.dot_general(k_now, fresh, (((0,), (0,)), ((), ())), precision=HIGH)  161 us
    dot_general x144, matrix products, step(): jnp.dot(q_now, state, precision=HIGH)  158 us
    reduce_scatter x1, waiting for transfers between devices, on_device(): lax.psum_scatter(jnp.dot(mixed_low, out_weight, preferred_element_type=jn...  143 us
  transfers between devices with their start and end apart: 9, of which 9 were waited for; matrix products, arithmetic and copies ran while one was open for 6% of the time, Pallas kernels for 0%

commit v1 on v0

v1 whole, which is shorter than its diff:
```python
from functools import partial

import jax
import jax.numpy as jnp
from jax import lax
from jax.experimental import pallas as pl
from jax.experimental.pallas import tpu as pltpu
from jax.sharding import PartitionSpec as P

DK = 128
DV = 256
CONV = 4
CHUNK = 128
LANES = 2 * DK + DV
WIDE = LANES + DV
BASE = 8
PRIOR = 16
F32 = jnp.float32
LOW = jnp.bfloat16


def dot(a, b):
    return lax.dot_general(a, b, (((1,), (0,)), ((), ())), preferred_element_type=F32)


def dot_rows(a, b):
    return lax.dot_general(a, b, (((1,), (1,)), ((), ())), preferred_element_type=F32)


def dot_cols(a, b):
    return lax.dot_general(a, b, (((0,), (0,)), ((), ())), preferred_element_type=F32)


def halves(a):
    high = a.astype(LOW)
    return high, (a - high.astype(F32)).astype(LOW)


def unit_lower_inverse(lows):
    size = lows[0].shape[0]
    row = lax.broadcasted_iota(jnp.int32, (size, size), 0)
    col = lax.broadcasted_iota(jnp.int32, (size, size), 1)
    eye = (row == col).astype(F32)
    near = (row // BASE) == (col // BASE)
    first = [jnp.where(near, -a, 0.0) for a in lows]
    powers = [p.astype(LOW) for p in first]
    inverse = [eye + p for p in first]
    span = 2
    while span < BASE:
        powers = [dot(p, p).astype(LOW) for p in powers]
        inverse = [t + dot(p, t.astype(LOW)) for p, t in zip(powers, inverse)]
        span *= 2
    span = BASE
    while span < size:
        band = ((row // (2 * span)) == (col // (2 * span))) & ((row // span) > (col // span))
        held = [t.astype(LOW) for t in inverse]
        moved = [dot(jnp.where(band, a, 0.0).astype(LOW), t).astype(LOW) for a, t in zip(lows, held)]
        inverse = [t - dot(h, m) for t, h, m in zip(inverse, held, moved)]
        span *= 2
    parts = [halves(t) for t in inverse]
    news = []
    for a, t, (t_high, t_low) in zip(lows, inverse, parts):
        a_high, a_low = halves(a)
        left = eye - t - (dot(a_high, t_high) + (dot(a_high, t_low) + dot(a_low, t_high)))
        news.append(t + dot(t_high, left.astype(LOW)))
    return news


def masks(marks, line):
    size = marks.shape[0]
    row = lax.broadcasted_iota(jnp.int32, (size, size), 0)
    col = lax.broadcasted_iota(jnp.int32, (size, size), 1)
    same = marks[:, 6:7] == line[0:1, :]
    return (row >= col) & same, (row > col) & same


def col_of(vals, kind, head, heads):
    at = kind * heads + head
    return vals[:, at : at + 1]


def rate_terms(logits, params, marks, heads):
    size = logits.shape[0]
    row = lax.broadcasted_iota(jnp.int32, (size, size), 0)
    col = lax.broadcasted_iota(jnp.int32, (size, size), 1)
    until = (row >= col).astype(LOW)
    shifted = logits + params[0:1, :]
    soft = jnp.maximum(shifted, 0.0) + jnp.log1p(jnp.exp(-jnp.abs(shifted)))
    decay = params[1:2, :] * soft
    high, rest = halves(decay)
    middle, small = halves(decay - high.astype(F32))
    grown = dot(until, high) + (dot(until, middle) + dot(until, small))
    start = jnp.exp(grown) * marks[:, 7:8]
    last = jnp.exp(grown[size - 1 : size, :] - grown) * marks[:, 8:9]
    lane = lax.broadcasted_iota(jnp.int32, logits.shape, 1)
    packed = pltpu.roll(logits, 4 * heads, 1)
    packed = jnp.where(lane < 4 * heads, pltpu.roll(last, 2 * heads, 1), packed)
    packed = jnp.where(lane < 3 * heads, pltpu.roll(start, heads, 1), packed)
    packed = jnp.where(lane < 2 * heads, grown, packed)
    packed = jnp.where(lane < heads, sigmoid(logits), packed)
    return packed, grown.T[heads : 2 * heads]


def sigmoid(x):
    return 1.0 / (1.0 + jnp.exp(-x))


def conv_sum(ext, cols, taps, at):
    size = cols.shape[0]
    total = ext[PRIOR : PRIOR + size, at : at + LANES] * taps[CONV - 1 : CONV, at : at + LANES]
    for back in range(1, CONV):
        moved = ext[PRIOR - back : PRIOR - back + size, at : at + LANES]
        tap = taps[CONV - 1 - back : CONV - back, at : at + LANES]
        total = total + (cols[:, back - 1 : back] * moved) * tap
    return total


def fwd_kernel(pick_ref, own_ref, got_ref, marks_ref, line_ref, mix_ref, rate_ref, first_ref, params_ref, taps_ref,
               gain_ref, state_in, tail_in, *refs):
    (mixed_ref, first_out, proj_ref, vals_ref, rows_ref, s_ref, t_ref, f_ref, o_ref,
     state, tail, ext) = refs[-12:]
    heads = state.shape[0]
    size = CHUNK

    @pl.when(pl.program_id(0) == 0)
    def _():
        state[...] = state_in[...]
        tail[...] = tail_in[...]

    hs = range(heads)
    marks = marks_ref[...]
    pick = pick_ref[0, 0]
    x = pick * own_ref[...].astype(F32) + (1.0 - pick) * got_ref[...].astype(F32)
    first = x * lax.rsqrt(jnp.mean(x * x, axis=1, keepdims=True) + 1e-05) * first_ref[...]
    first = first.astype(LOW)
    first_out[...] = first
    vals, grown = rate_terms(dot(first, rate_ref[...]), params_ref[...], marks, heads)
    vals_ref[...] = vals
    rows_ref[0:heads, :] = grown
    within, strict = masks(marks, line_ref[...])
    ext[0:PRIOR, :] = tail[...]
    for h in hs:
        at = h * LANES
        proj = dot(first, mix_ref[:, h * WIDE : (h + 1) * WIDE])
        proj_ref[:, h * WIDE : (h + 1) * WIDE] = proj
        ext[PRIOR : PRIOR + size, at : at + LANES] = proj[:, :LANES]
        tail[:, at : at + LANES] = proj[size - PRIOR :, :LANES]
    qs, ks, vs, betas, starts, lasts, fades = [], [], [], [], [], [], []
    for h in hs:
        summed = conv_sum(ext, marks, taps_ref, h * LANES)
        act = summed * sigmoid(summed)
        q = act[:, :DK]
        k = act[:, DK : 2 * DK]
        qs.append(q * (lax.rsqrt(jnp.sum(q * q, axis=1, keepdims=True) + 1e-06) * DK ** (-0.5)))
        ks.append(k * lax.rsqrt(jnp.sum(k * k, axis=1, keepdims=True) + 1e-06))
        vs.append(act[:, 2 * DK :])
        betas.append(col_of(vals, 0, h, heads))
        starts.append(col_of(vals, 2, h, heads))
        lasts.append(col_of(vals, 3, h, heads))
        spread = col_of(vals, 1, h, heads) - grown[h : h + 1, :]
        fades.append(jnp.exp(jnp.where(within, spread, -1e9)))
    stacks = [jnp.concatenate([q, k], axis=0).astype(LOW) for q, k in zip(qs, ks)]
    klows = [s[size:] for s in stacks]
    inner = [dot_rows(s, k) for s, k in zip(stacks, klows)]
    scores = [(i[:size] * m).astype(LOW) for i, m in zip(inner, fades)]
    lows = [jnp.where(strict, b * (i[size:] * m), 0.0) for b, i, m in zip(betas, inner, fades)]
    solve = [t.astype(LOW) for t in unit_lower_inverse(lows)]
    olds = [state[h] for h in hs]
    held = [s.astype(LOW) for s in olds]
    reads = [dot(q, s) for q, s in zip(stacks, held)]
    right = [(b * (v - e * r[size:])).astype(LOW) for b, v, e, r in zip(betas, vs, starts, reads)]
    fresh = [dot(t, x).astype(LOW) for t, x in zip(solve, right)]
    ends = [(l * k).astype(LOW) for l, k in zip(lasts, ks)]
    grows = [dot_cols(k, f) for k, f in zip(ends, fresh)]
    for h in hs:
        state[h] = starts[h][size - 1 : size, :] * olds[h] + grows[h]
    outs = [e * r[:size] + dot(p, f) for e, r, p, f in zip(starts, reads, scores, fresh)]
    gain = gain_ref[...]
    for h in hs:
        o = outs[h]
        gate = proj_ref[:, h * WIDE + LANES : (h + 1) * WIDE]
        scaled = o * lax.rsqrt(jnp.mean(o * o, axis=1, keepdims=True) + 1e-05) * gain
        mixed_ref[:, h * DV : (h + 1) * DV] = (scaled * (gate * sigmoid(gate))).astype(LOW)
        s_ref[0, h] = held[h]
        t_ref[0, h] = solve[h]
        f_ref[:, h * DV : (h + 1) * DV] = fresh[h]
        o_ref[:, h * DV : (h + 1) * DV] = o.astype(LOW)


def fold(x):
    return jnp.sum(x.reshape(x.shape[0] // 8, 8, x.shape[1]), axis=0)


def bwd_kernel(dmix_ref, prev_ref, proj_ref, marks_ref, line_ref, vals_ref, rows_ref, taps_ref, gain_ref,
               s_ref, t_ref, f_ref, o_ref,
               dproj_ref, dcols_ref, drows_ref, dtaps_ref, dgain_ref, dstate, ext, after,
               *, first, total_heads):
    heads = dstate.shape[0]
    size = CHUNK

    @pl.when(pl.program_id(0) == 0)
    def _():
        dstate[...] = jnp.zeros_like(dstate)
        after[...] = jnp.zeros_like(after)
        dtaps_ref[...] = jnp.zeros_like(dtaps_ref)
        dgain_ref[...] = jnp.zeros_like(dgain_ref)

    marks = marks_ref[...]
    vals = vals_ref[...]
    rows = rows_ref[...]
    within, strict = masks(marks, line_ref[...])
    gain = gain_ref[...]
    for h in range(heads):
        at = h * LANES
        ext[0:PRIOR, at : at + LANES] = prev_ref[:, h * WIDE : h * WIDE + LANES].astype(F32)
        ext[PRIOR : PRIOR + size, at : at + LANES] = proj_ref[:, h * WIDE : h * WIDE + LANES].astype(F32)
    hs = range(heads)
    summed = [conv_sum(ext, marks, taps_ref, h * LANES) for h in hs]
    sig = [sigmoid(s) for s in summed]
    act = [s * g for s, g in zip(summed, sig)]
    slope = [g * (1.0 + s * (1.0 - g)) for s, g in zip(summed, sig)]
    rq = [lax.rsqrt(jnp.sum(a[:, :DK] * a[:, :DK], axis=1, keepdims=True) + 1e-06) for a in act]
    rk = [lax.rsqrt(jnp.sum(a[:, DK : 2 * DK] * a[:, DK : 2 * DK], axis=1, keepdims=True) + 1e-06) for a in act]
    qn = [a[:, :DK] * r for a, r in zip(act, rq)]
    ks = [a[:, DK : 2 * DK] * r for a, r in zip(act, rk)]
    vs = [a[:, 2 * DK :] for a in act]
    betas = [col_of(vals, 0, first + h, total_heads) for h in hs]
    starts = [col_of(vals, 2, first + h, total_heads) for h in hs]
    lasts = [col_of(vals, 3, first + h, total_heads) for h in hs]
    fades = [
        jnp.exp(jnp.where(within, col_of(vals, 1, first + h, total_heads) - rows[first + h : first + h + 1, :], -1e9)) for h in hs
    ]
    stacks = [jnp.concatenate([q * DK ** (-0.5), k], axis=0).astype(LOW) for q, k in zip(qn, ks)]
    qlows = [s[:size] for s in stacks]
    klows = [s[size:] for s in stacks]
    inner = [dot_rows(s, k) for s, k in zip(stacks, klows)]
    scores = [i[:size] * m for i, m in zip(inner, fades)]
    pairs = [jnp.where(strict, i[size:] * m, 0.0) for i, m in zip(inner, fades)]
    held = [s_ref[0, h] for h in hs]
    reads = [dot(q, s) for q, s in zip(stacks, held)]
    douts = []
    for h in hs:
        o = o_ref[:, h * DV : (h + 1) * DV].astype(F32)
        gate = proj_ref[:, h * WIDE + LANES : (h + 1) * WIDE].astype(F32)
        dmix = dmix_ref[:, h * DV : (h + 1) * DV].astype(F32)
        r = lax.rsqrt(jnp.mean(o * o, axis=1, keepdims=True) + 1e-05)
        g = sigmoid(gate)
        on = o * r
        u = dmix * (gate * g)
        dgain_ref[...] += fold(u * on)
        dgate = (dmix * on * gain) * (g * (1.0 + gate * (1.0 - g)))
        dproj_ref[:, h * WIDE + LANES : (h + 1) * WIDE] = dgate.astype(LOW)
        w = u * gain
        douts.append(r * (w - on * jnp.mean(w * on, axis=1, keepdims=True)))
    dlows = [d.astype(LOW) for d in douts]
    dnexts = [dstate[h] for h in hs]
    dheld = [d.astype(LOW) for d in dnexts]
    ends = [(l * k).astype(LOW) for l, k in zip(lasts, ks)]
    solve = [t_ref[0, h] for h in hs]
    fresh = [f_ref[:, h * DV : (h + 1) * DV] for h in hs]
    dfresh = [dot_cols(p.astype(LOW), d) + dot(k, s) for p, d, k, s in zip(scores, dlows, ends, dheld)]
    dright = [dot_cols(t, d.astype(LOW)) for t, d in zip(solve, dfresh)]
    outer = [
        dot_rows(jnp.concatenate([d, x.astype(LOW)], axis=0), f)
        for d, x, f in zip(dlows, dright, fresh)
    ]
    scaled = [b * x for b, x in zip(betas, dright)]
    dreads = [
        jnp.concatenate([e * d, -e * x], axis=0).astype(LOW) for e, d, x in zip(starts, douts, scaled)
    ]
    for h in hs:
        dstate[h] = starts[h][size - 1 : size, :] * dnexts[h] + dot_cols(stacks[h], dreads[h])
    dqk = [dot_rows(d, s) for d, s in zip(dreads, held)]
    dend = [dot_rows(f, s) for f, s in zip(fresh, dheld)]
    last_row = lax.broadcasted_iota(jnp.int32, (size, 1), 0) == size - 1
    dscore = [o[:size] * m for o, m in zip(outer, fades)]
    dpair = [-o[size:] for o in outer]
    dinner = [jnp.where(strict, b * d * m, 0.0) for b, d, m in zip(betas, dpair, fades)]
    dq_in = [dot(d.astype(LOW), k) for d, k in zip(dscore, klows)]
    dk_in = [
        dot_cols(d.astype(LOW), q) + dot((i + i.T).astype(LOW), k)
        for d, q, i, k in zip(dscore, qlows, dinner, klows)
    ]
    for h in hs:
        e, b, dr, y, z = starts[h], betas[h], dright[h], reads[h][:size], reads[h][size:]
        weights = scores[h] * outer[h][:size] + b * pairs[h] * dpair[h]
        dbeta = jnp.sum(dr * (vs[h] - e * z), axis=1, keepdims=True) + jnp.sum(
            dpair[h] * pairs[h], axis=1, keepdims=True
        )
        dstart = jnp.sum(douts[h] * y - scaled[h] * z, axis=1, keepdims=True)
        through = jnp.sum(dnexts[h] * held[h].astype(F32))
        dstart = dstart + jnp.where(last_row, through, 0.0)
        dlast = jnp.sum(ks[h] * dend[h], axis=1, keepdims=True)
        at = h
        dcols_ref[:, at : at + 1] = dbeta
        dcols_ref[:, heads + at : heads + at + 1] = jnp.sum(weights, axis=1, keepdims=True)
        dcols_ref[:, 2 * heads + at : 2 * heads + at + 1] = dstart
        dcols_ref[:, 3 * heads + at : 3 * heads + at + 1] = dlast
        drows_ref[h : h + 1, :] = jnp.sum(weights, axis=0, keepdims=True)
    for h in hs:
        dq = dqk[h][:size] + dq_in[h]
        dk = dqk[h][size:] + dk_in[h] + lasts[h] * dend[h]
        dv = scaled[h]
        dq = (rq[h] * DK ** (-0.5)) * (dq - qn[h] * jnp.sum(dq * qn[h], axis=1, keepdims=True))
        dk = rk[h] * (dk - ks[h] * jnp.sum(dk * ks[h], axis=1, keepdims=True))
        at = h * LANES
        dsum = jnp.concatenate([dq, dk, dv], axis=1) * slope[h]
        after[0:size, at : at + LANES] = dsum
        here = slice(at, at + LANES)
        dproj = dsum * taps_ref[CONV - 1 : CONV, here]
        dtaps_ref[CONV - 1, :, here] += fold(dsum * ext[PRIOR : PRIOR + size, here])
        for back in range(1, CONV):
            moved = ext[PRIOR - back : PRIOR - back + size, here]
            dtaps_ref[CONV - 1 - back, :, here] += fold((marks[:, back - 1 : back] * moved) * dsum)
            later = after[back : back + size, here]
            dproj = dproj + (marks[:, 2 + back : 3 + back] * later) * taps_ref[CONV - 1 - back : CONV - back, here]
        dproj_ref[:, h * WIDE : h * WIDE + LANES] = dproj.astype(LOW)
        after[size : size + 8, here] = dsum[0:8]


PARAMS = pltpu.CompilerParams(
    dimension_semantics=("arbitrary",), vmem_limit_bytes=56 * 1024 * 1024
)


def fixed(shape):
    return pl.BlockSpec(shape, lambda i: (0,) * len(shape), pipeline_mode=pl.Buffered(1))


def cost(total, heads):
    return pl.CostEstimate(
        flops=10_000_000 * total * heads, bytes_accessed=total * heads * 8192, transcendentals=0
    )


def mixer_fwd(pick, x, got, marks, line, weights, state, tail, kept, at):
    mix_w, rate_w, first_gain, params, taps, gain = weights
    total, width = line.shape[1], x.shape[1]
    heads = mix_w.shape[1] // WIDE
    chunks = total // CHUNK
    rows_at = lambda i: (at + i, 0)
    blocks_at = lambda i: (at + i, 0, 0, 0)
    whole = [
        (pl.BlockSpec((CHUNK, width), rows_at), (total, width), LOW),
        (pl.BlockSpec((CHUNK, heads * WIDE), rows_at), (total, heads * WIDE), F32),
        (pl.BlockSpec((CHUNK, 128), rows_at), (total, 128), F32),
        (pl.BlockSpec((8, CHUNK), lambda i: (0, at + i)), (8, total), F32),
        (pl.BlockSpec((1, heads, DK, DV), blocks_at), (chunks, heads, DK, DV), LOW),
        (pl.BlockSpec((1, heads, CHUNK, CHUNK), blocks_at), (chunks, heads, CHUNK, CHUNK), LOW),
        (pl.BlockSpec((CHUNK, heads * DV), rows_at), (total, heads * DV), LOW),
        (pl.BlockSpec((CHUNK, heads * DV), rows_at), (total, heads * DV), LOW),
    ]
    in_specs = [
        pl.BlockSpec(memory_space=pltpu.SMEM),
        pl.BlockSpec((CHUNK, width), lambda i: (i, 0)),
        pl.BlockSpec((CHUNK, width), lambda i: (i, 0)),
        pl.BlockSpec((CHUNK, marks.shape[1]), rows_at),
        pl.BlockSpec((8, CHUNK), lambda i: (0, at + i)),
        fixed(mix_w.shape),
        fixed(rate_w.shape),
        fixed(first_gain.shape),
        fixed(params.shape),
        fixed(taps.shape),
        fixed(gain.shape),
        fixed((heads, DK, DV)),
        fixed((PRIOR, heads * LANES)),
    ]
    out = pl.pallas_call(
        fwd_kernel,
        grid=(x.shape[0] // CHUNK,),
        in_specs=in_specs + [pl.BlockSpec(memory_space=pl.ANY)] * len(kept),
        out_specs=[pl.BlockSpec((CHUNK, heads * DV), lambda i: (i, 0))]
        + [w[0] for w in whole]
        + [
            pl.BlockSpec((heads, DK, DV), lambda i: (0, 0, 0)),
            pl.BlockSpec((PRIOR, heads * LANES), lambda i: (0, 0)),
        ],
        out_shape=[jax.ShapeDtypeStruct((x.shape[0], heads * DV), LOW)]
        + [jax.ShapeDtypeStruct(w[1], w[2]) for w in whole]
        + [
            jax.ShapeDtypeStruct((heads, DK, DV), F32),
            jax.ShapeDtypeStruct((PRIOR, heads * LANES), F32),
        ],
        scratch_shapes=[pltpu.VMEM((CHUNK + PRIOR, heads * LANES), F32)],
        input_output_aliases={len(in_specs) + n: 1 + n for n in range(len(kept))},
        compiler_params=PARAMS,
        cost_estimate=cost(x.shape[0], heads),
        name="mixer_forward",
    )(pick, x, got, marks, line, mix_w, rate_w, first_gain, params, taps, gain, state, tail, *kept)
    return out[0], out[1:9], out[9], out[10]


def mixer_bwd(dmixed, marks, line, taps, gain, kept, group, groups):
    proj, vals, rows, states, solves, fresh, outs = kept
    total = proj.shape[0]
    whole = proj.shape[1] // WIDE
    heads = whole // groups
    chunks = total // CHUNK
    per = CHUNK // PRIOR
    at = lambda i: chunks - 1 - i
    return pl.pallas_call(
        partial(bwd_kernel, first=group * heads, total_heads=whole),
        grid=(chunks,),
        in_specs=[
            pl.BlockSpec((CHUNK, heads * DV), lambda i: (at(i), group)),
            pl.BlockSpec((PRIOR, heads * WIDE), lambda i: (jnp.maximum(at(i) * per - 1, 0), group)),
            pl.BlockSpec((CHUNK, heads * WIDE), lambda i: (at(i), group)),
            pl.BlockSpec((CHUNK, marks.shape[1]), lambda i: (at(i), 0)),
            pl.BlockSpec((8, CHUNK), lambda i: (0, at(i))),
            pl.BlockSpec((CHUNK, 128), lambda i: (at(i), 0)),
            pl.BlockSpec((rows.shape[0], CHUNK), lambda i: (0, at(i))),
            pl.BlockSpec((CONV, heads * LANES), lambda i: (0, group)),
            pl.BlockSpec((1, DV), lambda i: (0, 0)),
            pl.BlockSpec((1, heads, DK, DV), lambda i: (at(i), group, 0, 0)),
            pl.BlockSpec((1, heads, CHUNK, CHUNK), lambda i: (at(i), group, 0, 0)),
            pl.BlockSpec((CHUNK, heads * DV), lambda i: (at(i), group)),
            pl.BlockSpec((CHUNK, heads * DV), lambda i: (at(i), group)),
        ],
        out_specs=[
            pl.BlockSpec((CHUNK, heads * WIDE), lambda i: (at(i), 0)),
            pl.BlockSpec((CHUNK, 4 * heads), lambda i: (at(i), 0)),
            pl.BlockSpec((8, CHUNK), lambda i: (0, at(i))),
            pl.BlockSpec((CONV, 8, heads * LANES), lambda i: (0, 0, 0)),
            pl.BlockSpec((8, DV), lambda i: (0, 0)),
        ],
        out_shape=[
            jax.ShapeDtypeStruct((total, heads * WIDE), LOW),
            jax.ShapeDtypeStruct((total, 4 * heads), F32),
            jax.ShapeDtypeStruct((8, total), F32),
            jax.ShapeDtypeStruct((CONV, 8, heads * LANES), F32),
            jax.ShapeDtypeStruct((8, DV), F32),
        ],
        scratch_shapes=[
            pltpu.VMEM((heads, DK, DV), F32),
            pltpu.VMEM((CHUNK + PRIOR, heads * LANES), F32),
            pltpu.VMEM((CHUNK + 8, heads * LANES), F32),
        ],
        compiler_params=PARAMS,
        cost_estimate=cost(total, heads),
        name="mixer_backward",
    )(dmixed, proj, proj, marks, line, vals, rows, taps, gain, states, solves, fresh, outs)


def merge_back(parts, heads):
    each = heads // len(parts)
    cut = [[p[1][:, k * each : (k + 1) * each] for p in parts] for k in range(4)]
    dbeta, dgrown, dstart, dlast = [jnp.concatenate(c, axis=1) for c in cut]
    dgrown = dgrown - jnp.concatenate([p[2][:each] for p in parts], axis=0).T
    dtaps = jnp.concatenate([jnp.sum(p[3], axis=1) for p in parts], axis=1)
    dgain = sum(jnp.sum(p[4], axis=0) for p in parts)
    return (dbeta, dgrown, dstart, dlast), dtaps, dgain


def prep(rates, decay_log, decay_bias, segment):
    total = rates.shape[0]
    heads = decay_log.shape[0]
    chunks = total // CHUNK
    pieces = rates.reshape(total, heads, 2)
    beta = jax.nn.sigmoid(pieces[..., 0])
    decay = -jnp.exp(decay_log) * jax.nn.softplus(pieces[..., 1] + decay_bias)
    order = jnp.arange(CHUNK)
    until = (order[:, None] >= order[None, :]).astype(F32)
    grown = jnp.einsum(
        "ij,njh->nih", until, decay.reshape(chunks, CHUNK, heads), precision=lax.Precision.HIGHEST
    )
    seg = segment.reshape(chunks, CHUNK)
    before = jnp.concatenate([jnp.full((1,), -1, jnp.int32), seg[:-1, -1]])
    carried = (seg == before[:, None])[:, :, None]
    start = jnp.where(carried, jnp.exp(grown), 0.0)
    ending = (seg == seg[:, -1:])[:, :, None]
    last = jnp.where(ending, jnp.exp(jnp.where(ending, grown[:, -1:] - grown, 0.0)), 0.0)
    return (
        beta,
        grown.reshape(total, heads),
        start.reshape(total, heads),
        last.reshape(total, heads),
    )


def tables(segment):
    total = segment.shape[0]
    seg = segment.reshape(-1, CHUNK)
    before = jnp.concatenate([jnp.full((1,), -1, jnp.int32), seg[:-1, -1]])
    marks = []
    for back in range(1, CONV):
        prior = jnp.pad(segment, (back, 0), constant_values=-1)[:total]
        marks.append(prior == segment)
    for back in range(1, CONV):
        later = jnp.pad(segment, (0, back), constant_values=-1)[back:]
        marks.append(later == segment)
    marks.append(segment)
    marks.append((seg == before[:, None]).reshape(total))
    marks.append((seg == seg[:, -1:]).reshape(total))
    marks += [jnp.zeros((total,), F32)] * 7
    marks = jnp.stack([m.astype(F32) for m in marks], axis=1)
    return marks, jnp.broadcast_to(segment.astype(F32)[None], (8, total))


def mixer_weights(mix_w, rate_w, first_gain, decay_log, decay_bias, taps, gain):
    heads = decay_log.shape[0]
    paired_w = rate_w.reshape(-1, heads, 2)
    filled = jnp.concatenate([paired_w[..., 0], paired_w[..., 1]], axis=1)
    filled = jnp.pad(filled, ((0, 0), (0, 128 - 2 * heads)))
    params = jnp.zeros((8, 128), F32)
    params = params.at[0, heads : 2 * heads].set(decay_bias)
    params = params.at[1, heads : 2 * heads].set(-jnp.exp(decay_log))
    return mix_w, filled, first_gain[None], params, taps, gain[None]


def rates_back(vals, decay_log, decay_bias, segment, grads):
    heads = decay_log.shape[0]
    logits = vals[:, 4 * heads : 6 * heads].reshape(-1, 2, heads).transpose(0, 2, 1)
    rates = logits.reshape(-1, 2 * heads)
    back = jax.vjp(lambda r, l, b: prep(r, l, b, segment), rates, decay_log, decay_bias)[1]
    return back(grads)


def cross(left, right):
    return lax.dot_general(
        left, right, (((0,), (0,)), ((), ())), preferred_element_type=F32
    )


def wide_dot(left, right):
    return jnp.dot(left, right, preferred_element_type=F32)


def back_dot(grad, weight):
    return lax.dot_general(
        grad, weight, (((1,), (1,)), ((), ())), preferred_element_type=F32
    )


def norm_parts(value):
    return lax.rsqrt(jnp.mean(value * value, axis=-1, keepdims=True) + 1e-05)


def norm_back(value, scale, gain, grad):
    u = gain * grad
    part = scale * u - value * (scale * scale * scale) * jnp.mean(u * value, axis=-1, keepdims=True)
    return part, jnp.sum(grad * value * scale, axis=0)


def layout(lengths, capacity):
    bounds = jnp.cumsum(lengths)
    position = jnp.arange(capacity, dtype=jnp.int32)
    segment = jnp.sum((position[:, None] >= bounds[None, :]).astype(jnp.int32), axis=1)
    live = (position < bounds[-1]).astype(F32)[:, None]
    return segment, live


class Pair:
    def __init__(self, groups):
        self.here = lax.axis_index("tensor")
        self.core = lax.axis_index("dp") % 2
        self.side = (lax.axis_index("dp") // 2) % 2
        self.cores = [(i, i ^ 1) for i in range(groups)]
        self.sides = [(i, i ^ 2) for i in range(groups)]
        self.groups = groups

    def across(self, value):
        return lax.ppermute(value, "tensor", [(0, 1), (1, 0)])

    def beside(self, value):
        return lax.ppermute(value, "dp", self.cores)

    def along(self, value):
        return lax.ppermute(value, "dp", self.sides)

    def part(self, value, which):
        size = value.shape[0] // 2
        return lax.dynamic_slice_in_dim(value, which * size, size, 0)

    def join(self, mine, other, which):
        low = jnp.where(which == 0, mine, other)
        return jnp.concatenate([low, jnp.where(which == 0, other, mine)], axis=0)

    def halve(self, value):
        mine = self.part(value, self.core).astype(F32)
        got = self.beside(self.part(value, 1 - self.core)).astype(F32)
        return (mine + got).astype(LOW)

    def quarter(self, half):
        mine = self.part(half, self.side).astype(F32)
        got = self.along(self.part(half, 1 - self.side)).astype(F32)
        return (mine + got).astype(LOW)

    def sum(self, values, turn, alike=2):
        orders = []
        for c in range(alike):
            order = list(range(c, self.groups, alike))
            order = order[turn:] + order[:turn]
            orders.append(order)
        return lax.psum(values, "dp", axis_index_groups=orders)

    def halves(self, values):
        return [self.join(v, self.along(v), self.side) for v in values]

    def everywhere(self, value):
        step = 1
        while step < self.groups:
            value = value + lax.ppermute(value, "dp", [(i, i ^ step) for i in range(self.groups)])
            step *= 2
        return value

    def whole(self, values):
        return [self.join(v, self.beside(v), self.core).astype(F32) for v in values]


def feed_forward(residual, live, second_gain, gate_w, up_w, down_w, out_grad):
    scale = norm_parts(residual)
    second_low = (residual * scale * second_gain).astype(LOW)
    gate = wide_dot(second_low, gate_w)
    up = wide_dot(second_low, up_w)
    sigma = jax.nn.sigmoid(gate)
    gated = gate * sigma
    hidden = (gated * up).astype(LOW)
    block_out = (residual + live * wide_dot(hidden, down_w)).astype(LOW)
    ffn_grad = (live * out_grad).astype(LOW)
    hidden_grad = back_dot(ffn_grad, down_w)
    gate_grad = (hidden_grad * up * (sigma * (1.0 + gate * (1.0 - sigma)))).astype(LOW)
    up_grad = (hidden_grad * gated).astype(LOW)
    second_sum = back_dot(gate_grad, gate_w) + back_dot(up_grad, up_w)
    part, gain_part = norm_back(residual, scale, second_gain, second_sum)
    residual_grad = out_grad + part
    pieces = (second_low, hidden, ffn_grad, gate_grad, up_grad)
    return block_out, residual_grad, gain_part, pieces


def tied(*values):
    return lax.optimization_barrier(values)


def paired(
    tokens, seq_lengths, first_gain, mix_weight, rate_weight, conv_weight, decay_log, decay_bias,
    out_gain, out_weight, second_gain, gate_weight, up_weight, down_weight, cotangent,
):
    rows = tokens.shape[0]
    capacity = rows * 2
    move = Pair(lax.axis_size("dp"))
    here = move.here
    heads = decay_log.shape[0]
    cuts = 3 if rows % (3 * CHUNK) == 0 else 1
    piece = rows // cuts
    own = [tokens[j * piece : (j + 1) * piece] for j in range(cuts)]
    got = [move.across(own[0])]
    for j in range(1, cuts):
        got[-1], own[j] = tied(got[-1], own[j])
        got.append(move.across(own[j]))
    gate_src, up_src, down_src, last_got = tied(gate_weight, up_weight, down_weight, got[-1])
    got[-1] = last_got
    fetched = [
        move.across(move.part(move.part(w, move.core), move.side))
        for w in (gate_src, up_src, down_src)
    ]
    segment, live_all = layout(seq_lengths[0], capacity)
    live = lax.dynamic_slice_in_dim(live_all, here * rows, rows, 0)
    marks, line = tables(segment)
    weights = mixer_weights(
        mix_weight, rate_weight, first_gain, decay_log, decay_bias, conv_weight, out_gain
    )
    state = jnp.zeros((heads, DK, DV), F32)
    tail = jnp.zeros((PRIOR, heads * LANES), F32)
    first_half = (here == 0).astype(F32).reshape(1, 1)
    per = piece // CHUNK
    mixed, kept, attn_own, attn_got = [], (), [], []
    for p in range(2 * cuts):
        pick = first_half if p < cuts else 1.0 - first_half
        now, kept, state, tail = mixer_fwd(pick, own[p % cuts], got[p % cuts], marks, line, weights, state, tail, kept, p * per)
        mixed.append(now)
        if p == cuts:
            fetched, state = tied(fetched, state)
            fetched = [move.join(f, move.along(f), move.side) for f in fetched]
        if p >= cuts:
            low, high = wide_dot(mixed[p - cuts], out_weight), wide_dot(now, out_weight)
            attn_own.append(jnp.where(here == 0, low, high))
            attn_got.append(move.across(jnp.where(here == 0, high, low).astype(LOW)))
    fetched, mixed[-1] = tied(fetched, mixed[-1])
    others = [move.join(f, move.beside(f), move.core) for f in fetched]
    gate_w = jnp.concatenate([gate_weight, others[0]], axis=1)
    up_w = jnp.concatenate([up_weight, others[1]], axis=1)
    down_w = jnp.concatenate([down_weight, others[2]], axis=0)
    attn_got, gate_w, up_w, down_w = tied(attn_got, gate_w, up_w, down_w)
    attn = jnp.concatenate([a + g.astype(F32) for a, g in zip(attn_own, attn_got)], axis=0)
    first_rows, kept = kept[0], kept[1:]
    inputs = tokens.astype(F32)
    residual = inputs + live * attn

    width = gate_weight.shape[1]
    out_grad = cotangent.astype(F32)
    scale = norm_parts(residual)
    second_low = (residual * scale * second_gain).astype(LOW)
    gate = wide_dot(second_low, gate_w)
    up = wide_dot(second_low, up_w)
    sigma = jax.nn.sigmoid(gate)
    gated = gate * sigma
    hidden = (gated * up).astype(LOW)
    ffn_grad = (live * out_grad).astype(LOW)
    hidden_grad = back_dot(ffn_grad, down_w)
    gate_grad = (hidden_grad * up * (sigma * (1.0 + gate * (1.0 - sigma)))).astype(LOW)
    up_grad = (hidden_grad * gated).astype(LOW)
    grad_down = cross(hidden, ffn_grad).astype(LOW)
    down_halves = [move.halve(grad_down[:width]), move.halve(grad_down[width:])]
    gate_half = move.halve(cross(second_low, gate_grad).astype(LOW))
    up_half = move.halve(cross(second_low, up_grad).astype(LOW))
    down_mine, down_sent = [move.quarter(d) for d in down_halves]
    gate_in, up_in, down_mine, down_sent, gate_half, up_half = tied(
        gate_grad, up_grad, down_mine, down_sent, gate_half, up_half
    )
    gate_half, up_half = move.quarter(gate_half), move.quarter(up_half)
    down_sent = move.across(down_sent)
    gate_sent = move.across(gate_half[:, width:])
    up_sent = move.across(up_half[:, width:])
    second_sum = back_dot(gate_in, gate_w) + back_dot(up_in, up_w)
    part, second_part = norm_back(residual, scale, second_gain, second_sum)
    residual_grad = out_grad + part
    attn_low = (live * residual_grad).astype(LOW)
    attn_sent = move.across(attn_low)
    attn_low, hidden_in = tied(attn_low, hidden)
    block_out = (residual + live * wide_dot(hidden_in, down_w)).astype(LOW)
    mixed = jnp.concatenate(mixed, axis=0)
    gate_sum = gate_half[:, :width] + gate_sent
    up_sum = up_half[:, :width] + up_sent
    attn_sent, block_out, mixed, gate_sum, up_sum, down_sum = tied(
        attn_sent, block_out, mixed, gate_sum, up_sum, down_mine + down_sent
    )
    attn_grad = move.join(attn_low, attn_sent, here)
    dmixed = back_dot(attn_grad, out_weight).astype(LOW)
    grad_out = move.quarter(move.halve(cross(mixed, attn_grad).astype(LOW)))

    dmixed, sums_ffn_in = tied(dmixed, (gate_sum, up_sum, down_sum, grad_out))
    sums_ffn = move.sum(sums_ffn_in, 0, 4)
    back = mixer_bwd(dmixed, marks, line, conv_weight, out_gain[None], kept, 0, 1)
    back, sums_ffn = tied(back, sums_ffn)
    dproj = back[0]
    sums_ffn = move.halves(sums_ffn)
    dprep, dtaps, dgain = merge_back([back], heads)
    rates_grad, grad_log, grad_bias = rates_back(
        kept[1], decay_log, decay_bias, segment, dprep
    )
    rates_low = rates_grad.astype(LOW)

    def first_part(dproj, which):
        return back_dot(move.part(rates_low, which), rate_weight) + back_dot(
            move.part(dproj, which), mix_weight
        )

    theirs = first_part(dproj, 1 - here)
    theirs_low = theirs.astype(LOW)
    dproj, theirs_low = tied(dproj, theirs_low)
    sent = move.across(theirs_low)
    half = move.halve(cross(first_rows, dproj).astype(LOW))
    dproj, half, sums_ffn = tied(dproj, half, sums_ffn)
    (sum_mix,) = move.sum((half,), 1)
    mine = first_part(dproj, here)
    grad_rate = cross(rates_low, first_rows)
    token_own = inputs
    token_other = jnp.concatenate(got, axis=0).astype(F32)
    first_scale = norm_parts(token_own)
    first_part_gain = jnp.sum(mine * token_own * first_scale, axis=0) + jnp.sum(
        theirs * token_other * norm_parts(token_other), axis=0
    )
    model = first_gain.shape[0]
    thin = jnp.concatenate([dgain, grad_log, grad_bias])
    thin = jnp.pad(thin, (0, model - thin.shape[0]))
    small = jnp.concatenate(
        [first_part_gain[None], second_part[None], thin[None], grad_rate, dtaps.reshape(-1, model)]
    )
    small = move.everywhere(small)
    gains = small[:3] + move.across(small[:3])
    grad_first, grad_second, grad_outg = gains[0], gains[1], gains[2, :DV]
    grad_log = small[2, DV : DV + heads]
    grad_bias = small[2, DV + heads : DV + 2 * heads]
    grad_rate = small[3 : 3 + 2 * heads].T
    grad_conv = small[3 + 2 * heads :].reshape(dtaps.shape)

    grad_gate, grad_up, grad_down, grad_out = move.whole(sums_ffn)
    sent, grad_gate, grad_up, grad_down, grad_out = tied(
        sent, grad_gate, grad_up, grad_down, grad_out
    )
    input_part, _ = norm_back(inputs, first_scale, first_gain, mine + sent.astype(F32))
    tokens_grad = (residual_grad + input_part).astype(LOW)
    early = (
        block_out, tokens_grad, grad_first, grad_rate, grad_conv, grad_log, grad_bias,
        grad_outg, grad_second, grad_gate, grad_up, grad_down, grad_out,
    )
    early, sum_mix = tied(early, sum_mix)
    (grad_mix,) = move.whole((sum_mix,))
    (
        block_out, tokens_grad, grad_first, grad_rate, grad_conv, grad_log, grad_bias,
        grad_outg, grad_second, grad_gate, grad_up, grad_down, grad_out,
    ) = early
    return (
        block_out, tokens_grad, grad_first, grad_mix, grad_rate, grad_conv, grad_log, grad_bias,
        grad_outg, grad_out, grad_second, grad_gate, grad_up, grad_down,
    )


def spread(
    tokens, seq_lengths, first_gain, mix_weight, rate_weight, conv_weight, decay_log, decay_bias,
    out_gain, out_weight, second_gain, gate_weight, up_weight, down_weight, cotangent,
):
    rows = tokens.shape[0]
    capacity = rows * lax.axis_size("tensor")
    here = lax.axis_index("tensor")
    gather = lambda v, axis=0: lax.all_gather(v, "tensor", axis=axis, tiled=True)
    scatter = lambda v, axis=0: lax.psum_scatter(
        v.astype(LOW), "tensor", scatter_dimension=axis, tiled=True
    )
    inputs = tokens.astype(F32)
    first_scale = norm_parts(inputs)
    token_rows = gather(tokens)
    gate_w, up_w, down_w = gather(gate_weight, 1), gather(up_weight, 1), gather(down_weight)
    segment, live_all = layout(seq_lengths[0], capacity)
    live = lax.dynamic_slice_in_dim(live_all, here * rows, rows, 0)
    marks, line = tables(segment)
    weights = mixer_weights(
        mix_weight, rate_weight, first_gain, decay_log, decay_bias, conv_weight, out_gain
    )
    heads = decay_log.shape[0]
    state = jnp.zeros((heads, DK, DV), F32)
    tail = jnp.zeros((PRIOR, heads * LANES), F32)
    mixed, kept, state, tail = mixer_fwd(
        jnp.ones((1, 1), F32), token_rows, token_rows, marks, line, weights, state, tail, (), 0
    )
    first_rows, kept = kept[0], kept[1:]
    residual = inputs + live * scatter(wide_dot(mixed, out_weight)).astype(F32)
    out_grad = cotangent.astype(F32)
    block_out, residual_grad, second_part, pieces = feed_forward(
        residual, live, second_gain, gate_w, up_w, down_w, out_grad
    )
    second_low, hidden, ffn_grad, gate_grad, up_grad = pieces
    attn_grad = gather((live * residual_grad).astype(LOW))
    grad_gate = scatter(cross(second_low, gate_grad), 1)
    grad_up = scatter(cross(second_low, up_grad), 1)
    grad_down = scatter(cross(hidden, ffn_grad))
    dmixed = back_dot(attn_grad, out_weight).astype(LOW)
    grad_out = cross(mixed, attn_grad).astype(LOW)
    part = mixer_bwd(dmixed, marks, line, conv_weight, out_gain[None], kept, 0, 1)
    dproj = part[0]
    dprep, dtaps, dgain = merge_back([part], heads)
    rates_grad, grad_log, grad_bias = rates_back(kept[1], decay_log, decay_bias, segment, dprep)
    rates_low = rates_grad.astype(LOW)
    grad_mix = cross(first_rows, dproj).astype(LOW)
    grad_rate = cross(first_rows, rates_low)
    first_sum = scatter(back_dot(dproj, mix_weight) + back_dot(rates_low, rate_weight))
    input_part, first_gain_part = norm_back(inputs, first_scale, first_gain, first_sum.astype(F32))
    tokens_grad = (residual_grad + input_part).astype(LOW)
    grad_rate, grad_conv, grad_log, grad_bias = lax.psum(
        (grad_rate, dtaps, grad_log, grad_bias), "dp"
    )
    grad_first, grad_outg, grad_second = lax.psum(
        (first_gain_part, dgain, second_part), ("dp", "tensor")
    )
    grad_mix, grad_out, grad_gate, grad_up, grad_down = (
        g.astype(F32) for g in lax.psum((grad_mix, grad_out, grad_gate, grad_up, grad_down), "dp")
    )
    return (
        block_out, tokens_grad, grad_first, grad_mix, grad_rate, grad_conv, grad_log, grad_bias,
        grad_outg, grad_out, grad_second, grad_gate, grad_up, grad_down,
    )


def solution(mesh):
    placed = (
        P(("dp", "tensor"), None),
        P("dp", None),
        P(),
        P(None, "tensor"),
        P(None, "tensor"),
        P(None, "tensor"),
        P("tensor"),
        P("tensor"),
        P(),
        P("tensor", None),
        P(),
        P(None, "tensor"),
        P(None, "tensor"),
        P("tensor", None),
        P(("dp", "tensor"), None),
    )
    outer = mesh.shape["dp"]
    two = mesh.shape["tensor"] == 2 and outer >= 4 and outer & (outer - 1) == 0
    return jax.shard_map(
        paired if two else spread,
        mesh=mesh,
        in_specs=placed,
        out_specs=(
            P(("dp", "tensor"), None),
            P(("dp", "tensor"), None),
            P(),
            P(None, "tensor"),
            P(None, "tensor"),
            P(None, "tensor"),
            P("tensor"),
            P("tensor"),
            P(),
            P("tensor", None),
            P(),
            P(None, "tensor"),
            P(None, "tensor"),
            P("tensor", None),
        ),
        check_vma=False,
    )
```

time: 3430 us -> 1080 us (0.31)
  matrix products: 1150 us -> 252 us
  other arithmetic: 784 us -> 146 us
  local copies, waits for them, and re-layouts: 597 us -> 76 us
  waiting for transfers between devices: 746 us -> 278 us
  Pallas kernels: 0 us -> 260 us
  blocking collectives: 105 us -> 0 us
  starting transfers between devices: 0.37 us -> 39.2 us
    dot_general x637 -> x11, matrix products: 900 us -> 74.3 us  [the longest x9 73.2 us: wide_dot(): return jnp.dot(left, right, preferred_element_type=F32)]
    reduce_scatter x4 -> x0, waiting for transfers between devices: 338 us -> none  [the longest x1 143 us: on_device(): lax.psum_scatter(jnp.dot(mixed_low, out_weight, preferred_element_type=jn...]
    another operation x57 -> x5, other arithmetic: 282 us -> 2.21 us  [the longest x5 275 us: delta_head(): lax.linalg.triangular_solve(system, right, left_side=True, lower=True, un...]
    squeeze x288 -> x2, local copies, waits for them, and re-layouts: 271 us -> 2.46 us  [the longest x1 1.88 us: prep(): decay = -jnp.exp(decay_log) * jax.nn.softplus(pieces[..., 1] + decay_bias)]
    pallas_call x0 -> x7, Pallas kernels: none -> 260 us  [the longest x6 147 us: mixer_fwd(): pl.pallas_call(fwd_kernel, grid=(x.shape[0] // CHUNK,), in_specs=in_specs...]
    all_gather x4 -> x0, waiting for transfers between devices: 224 us -> none  [the longest x1 79.9 us: on_device(): second_rows = lax.all_gather(second_low, 'tensor', axis=0, tiled=True)]
    ppermute x0 -> x45, waiting for transfers between devices: none -> 217 us  [the longest x15 111 us: across(): return lax.ppermute(value, 'tensor', [(0, 1), (1, 0)])]
    reduce_sum x61 -> x5, other arithmetic: 152 us -> 9.74 us  [the longest x2 6.65 us: norm_parts(): return lax.rsqrt(jnp.mean(value * value, axis=-1, keepdims=True) + 1e-05)]
  transfers between devices with their start and end apart: 9 -> 47, of which waited for: 9 -> 20; matrix products, arithmetic and copies ran while one was open for 6% -> 26% of each run, Pallas kernels for 0% -> 24%
where the time goes in v1:
time: 1080 us; the launch traced here: 1070 us
  waiting for transfers between devices  278 us (26%)
  Pallas kernels  260 us (24%)
  matrix products  252 us (23%)
  other arithmetic  146 us (14%)
  local copies, waits for them, and re-layouts  76 us (7%)
  starting transfers between devices  39.2 us (4%)
  between operations  15.6 us (1%)
    pallas_call x6, Pallas kernels, mixer_fwd(): pl.pallas_call(fwd_kernel, grid=(x.shape[0] // CHUNK,), in_specs=in_specs...  147 us
    pallas_call x1, Pallas kernels, mixer_bwd(): pl.pallas_call(partial(bwd_kernel, first=group * heads, total_heads=whole...  113 us
    ppermute x15, waiting for transfers between devices, across(): return lax.ppermute(value, 'tensor', [(0, 1), (1, 0)])  111 us
    dot_general x8, matrix products, back_dot(): lax.dot_general(grad, weight, (((1,), (1,)), ((), ())), preferred_element...  102 us
    ppermute x12, waiting for transfers between devices, along(): return lax.ppermute(value, 'dp', self.sides)  90.1 us
    dot_general x6, matrix products, cross(): lax.dot_general(left, right, (((0,), (0,)), ((), ())), preferred_element_...  75.5 us
    dot_general x9, matrix products, wide_dot(): return jnp.dot(left, right, preferred_element_type=F32)  73.2 us
    psum x2, waiting for transfers between devices, sum(): return lax.psum(values, 'dp', axis_index_groups=orders)  60.5 us
  transfers between devices with their start and end apart: 47, of which 20 were waited for; matrix products, arithmetic and copies ran while one was open for 26% of the time, Pallas kernels for 24%

profile of v1, /device:TPU:0, one launch (start us, length us, event | category | flops | bytes accessed | tf_op | source)
XLA Modules:
  0.0 1066.1 jit_solution(11931532553108667632)
XLA Ops:
  27.7 9.6 collective-permute-done.got_ref
  42.9 24.2 %mixer_forward.6 = (bf16[512,1024]{1,0:T(8,128)(2,1)}, bf16[3072,1024]{1,0:T(8,128)(2,1)}, f32[3072,3072]{1,0:T(8,128)}, f32[3072,128]{1,0:T(8,128)}, f32[8,3072...) custom-call(f32[1,1]{1,0:T(1,128)} %bitcast.2.pick_ref, ...), custom_call_target="tpu_custom_call" | custom-call | flops 20480000000 | bytes 16777216 | tf_op jit(solution)/shard_map/mixer_forward/pallas_call | solution.py:368
  72.9 24.3 %mixer_forward.7 = (bf16[512,1024]{1,0:T(8,128)(2,1)}, bf16[3072,1024]{1,0:T(8,128)(2,1)}, f32[3072,3072]{1,0:T(8,128)}, f32[3072,128]{1,0:T(8,128)}, f32[8,3072...) custom-call(f32[1,1]{1,0:T(1,128)} %bitcast.2.pick_ref, ...), custom_call_target="tpu_custom_call", output_to_operand_aliasing={{1}: (13, {}), {2}: (14, {}), {3}: (15, {}), {4}: (16, {}),... | custom-call | flops 20480000000 | bytes 16777216 | tf_op jit(solution)/shard_map/mixer_forward/pallas_call | solution.py:368
  109.3 24.8 %mixer_forward.8 = (bf16[512,1024]{1,0:T(8,128)(2,1)}, bf16[3072,1024]{1,0:T(8,128)(2,1)}, f32[3072,3072]{1,0:T(8,128)}, f32[3072,128]{1,0:T(8,128)}, f32[8,3072...) custom-call(f32[1,1]{1,0:T(1,128)} %bitcast.2.pick_ref, ...), custom_call_target="tpu_custom_call", output_to_operand_aliasing={{1}: (13, {}), {2}: (14, {}), {3}: (15, {}), {4}: (16, {}),... | custom-call | flops 20480000000 | bytes 16777216 | tf_op jit(solution)/shard_map/mixer_forward/pallas_call | solution.py:368
  134.1 24.4 %mixer_forward.9 = (bf16[512,1024]{1,0:T(8,128)(2,1)}, bf16[3072,1024]{1,0:T(8,128)(2,1)}, f32[3072,3072]{1,0:T(8,128)}, f32[3072,128]{1,0:T(8,128)}, f32[8,3072...) custom-call(f32[1,1]{1,0:T(1,128)S(6)} %sub.60.pick_ref, ...), custom_call_target="tpu_custom_call", output_to_operand_aliasing={{1}: (13, {}), {2}: (14, {}), {3}: (15, {}), {4}: (16, {}),... | custom-call | flops 20480000000 | bytes 16777216 | tf_op jit(solution)/shard_map/mixer_forward/pallas_call | solution.py:368
  162.2 24.3 %mixer_forward.10 = (bf16[512,1024]{1,0:T(8,128)(2,1)}, bf16[3072,1024]{1,0:T(8,128)(2,1)}, f32[3072,3072]{1,0:T(8,128)}, f32[3072,128]{1,0:T(8,128)}, f32[8,307...) custom-call(f32[1,1]{1,0:T(1,128)S(6)} %sub.60.pick_ref, ...), custom_call_target="tpu_custom_call", output_to_operand_aliasing={{1}: (13, {}), {2}: (14, {}), {3}: (15, {}), {4}: (16, {}),... | custom-call | flops 20480000000 | bytes 16777216 | tf_op jit(solution)/shard_map/mixer_forward/pallas_call | solution.py:368
  186.5 24.6 %mixer_forward.11 = (bf16[512,1024]{1,0:T(8,128)(2,1)}, bf16[3072,1024]{1,0:T(8,128)(2,1)}, f32[3072,3072]{1,0:T(8,128)}, f32[3072,128]{1,0:T(8,128)}, f32[8,307...) custom-call(f32[1,1]{1,0:T(1,128)S(6)} %sub.60.pick_ref, ...), custom_call_target="tpu_custom_call", output_to_operand_aliasing={{1}: (13, {}), {2}: (14, {}), {3}: (15, {}), {4}: (16, {}),... | custom-call | flops 20480000000 | bytes 16777216 | tf_op jit(solution)/shard_map/mixer_forward/pallas_call | solution.py:368
  233.9 5.4 pad_maximum_fusion.1
  239.3 5.8 maximum_maximum_fusion.1
  245.1 16.3 %maximum_maximum_fusion = bf16[1024,2816]{1,0:T(8,128)(2,1)} fusion(bf16[512,1408]{1,0:T(8,128)(2,1)S(1)} %copy-done.24, bf16[512,1408]{1,0:T(8,128)(2,1)S(1)} %copy-done.23, bf16[1024,1408]{1,0:T(8,128)(2,1)} %param.30), kind=kLoop, calls=%fused_computation.41 | loop fusion | flops 17301504 | bytes 11534336 | tf_op jit(solution)/shard_map/concatenate | solution.py:680
  261.4 5.9 collective-permute-done.8
  267.3 22.1 %collective-permute-done.7 = bf16[512,1024]{1,0:T(8,128)(2,1)} collective-permute-done((bf16[512,1024]{1,0:T(8,128)(2,1)}, bf16[512,1024]{1,0:T(8,128)(2,1)}, u32[]{:S(2)}, u32[]{:S(2)}) %collective-permute-start.7) | collective-permute-done | bytes 1048608 | tf_op jit(solution)/shard_map/ppermute | solution.py:562
  295.6 4.5 multiply_reduce_fusion.2
  305.0 11.9 %fusion.94 = f32[1536,2816]{1,0:T(8,128)} fusion(bf16[1536,1024]{1,0:T(8,128)(2,1)S(1)} %multiply_convert_fusion.4, bf16[1024,2816]{1,0:T(8,128)(2,1)S(1)} %bitcast.146), kind=kOutput, calls=%fused_computation.259 | convolution fusion | flops 8858370048 | bytes 26214400 | tf_op jit(solution)/shard_map/dot_general | solution.py:525
  316.9 14.8 %fusion.32 = f32[1536,2816]{1,0:T(8,128)} fusion(bf16[2816,1024]{1,0:T(8,128)(2,1)S(1)} %bitcast.144, bf16[1536,1024]{1,0:T(8,128)(2,1)} %param.33, f32[1536]{0:T(1024)S(1)} %copy-done.47), kind=kOutput, calls=%fused_computation.112 | convolution fusion | flops 8863088640 | bytes 26220544 | tf_op jit(solution)/shard_map/dot_general | solution.py:529
  331.7 31.8 %multiply_convert_fusion = (bf16[1536,2816]{1,0:T(8,128)(2,1)}, bf16[1536,2816]{1,0:T(8,128)(2,1)}, bf16[1536,2816]{1,0:T(8,128)(2,1)}) fusion(f32[1536,2816]{1,0:T(8,128)} %fusion.94, f32[1536,2816]{1,0:T(8,128)} %fusion.32, bf16[1536,1024]{1,0:T(8,128)(2,1)} %copy-done.28, bf16[1024,2816]{1,0:T(8,128)(2,1)} %maximum_maximum_fusion.1), kind=kOutput, calls=%fused_computation | convolution fusion | flops 8923250688 | bytes 69468160 | tf_op jit(solution)/shard_map/dot_general | solution.py:525
  363.5 13.5 %convolution_convert_fusion = bf16[1024,2816]{1,0:T(8,128)(2,1)S(1)} fusion(bf16[1536,1024]{1,0:T(8,128)(2,1)} %copy-done.28, bf16[1536,2816]{1,0:T(8,128)(2,1)} %get-tuple-element.262), kind=kOutput, calls=%fused_computation.46 | convolution fusion | flops 8861253632 | bytes 17563648 | tf_op jit(solution)/shard_map/dot_general | solution.py:519
  380.0 12.1 %convolution_convert_fusion.4 = bf16[2816,1024]{1,0:T(8,128)(2,1)S(1)} fusion(bf16[1536,2816]{1,0:T(8,128)(2,1)} %get-tuple-element.263, bf16[1536,1024]{1,0:T(8,128)(2,1)S(1)} %copy-done.33, f32[1536]{0:T(1024)S(1)} %copy-done.47), kind=kOutput, calls=%fused_computation.50 | convolution fusion | flops 8865972224 | bytes 17569792 | tf_op jit(solution)/shard_map/dot_general | solution.py:519
  394.6 12.9 %convolution_convert_fusion.1 = bf16[1024,2816]{1,0:T(8,128)(2,1)S(1)} fusion(bf16[1536,1024]{1,0:T(8,128)(2,1)S(1)} %copy-done.29, bf16[1536,2816]{1,0:T(8,128)(2,1)} %get-tuple-element.261), kind=kOutput, calls=%fused_computation.47 | convolution fusion | flops 8861253632 | bytes 17563648 | tf_op jit(solution)/shard_map/dot_general | solution.py:519
  419.0 12.0 %collective-permute-done.18 = bf16[352,1024]{1,0:T(8,128)(2,1)S(1)} collective-permute-done((bf16[352,1024]{1,0:T(8,128)(2,1)S(1)}, bf16[352,1024]{1,0:T(8,128)(2,1)S(1)}, u32[]{:S(2)}, u32[]{:S(2)}) %collective-permute-start.18) | collective-permute-done | bytes 720928 | tf_op jit(solution)/shard_map/ppermute | solution.py:568
  431.2 13.9 %collective-permute-done.16 = bf16[352,1024]{1,0:T(8,128)(2,1)S(1)} collective-permute-done((bf16[352,1024]{1,0:T(8,128)(2,1)S(1)}, bf16[352,1024]{1,0:T(8,128)(2,1)S(1)}, u32[]{:S(2)}, u32[]{:S(2)}) %collective-permute-start.16) | collective-permute-done | bytes 720928 | tf_op jit(solution)/shard_map/ppermute | solution.py:568
  454.7 13.2 %fusion.95 = f32[1536,1024]{1,0:T(8,128)} fusion(bf16[1536,2816]{1,0:T(8,128)(2,1)} %get-tuple-element.262, bf16[1024,2816]{1,0:T(8,128)(2,1)S(1)} %bitcast.148), kind=kOutput, calls=%fused_computation.260 | convolution fusion | flops 8858370048 | bytes 20709376 | tf_op jit(solution)/shard_map/dot_general | solution.py:529
  467.9 18.0 %multiply_reduce_fusion = (f32[1024]{0:T(1024)}, f32[1536]{0:T(1024)S(1)}, f32[1536,1024]{1,0:T(8,128)}) fusion(f32[1536,1024]{1,0:T(8,128)S(1)} %bitcast.134, f32[1536]{0:T(1024)S(1)} %get-tuple-element.411, f32[1024]{0:T(1024)S(1)} %copy-done.55, f32[1536,1024]{1,0:T(8,128)} %fusion.95, bf16[1536,2816]{1,0:T(8,128)(2,1)} %get-tuple-element.261, ...), kind=kOutput, calls=%fused_computation.33 | convolution fusion | flops 8869378048 | bytes 33312768 | tf_op jit(solution)/shard_map/dot_general | solution.py:529
  485.9 6.9 multiply_convert_fusion.3
  498.2 16.7 %collective-permute-done.22 = bf16[256,2816]{1,0:T(8,128)(2,1)} collective-permute-done((bf16[256,2816]{1,0:T(8,128)(2,1)}, bf16[256,2816]{1,0:T(8,128)(2,1)}, u32[]{:S(2)}, u32[]{:S(2)}) %collective-permute-start.22) | collective-permute-done | bytes 1441824 | tf_op jit(solution)/shard_map/ppermute | solution.py:568
  518.3 14.4 %add_convert_fusion.1 = bf16[1536,1024]{1,0:T(8,128)(2,1)} fusion(f32[1536,1024]{1,0:T(8,128)S(1)} %bitcast.134, bf16[1536,2816]{1,0:T(8,128)(2,1)} %get-tuple-element.263, bf16[2816,1024]{1,0:T(8,128)(2,1)} %pad_maximum_fusion.1, f32[1536]{0:T(1024)S(1)} %copy-done.47), kind=kOutput, calls=%fused_computation.36 | convolution fusion | flops 8863088640 | bytes 23861248 | tf_op jit(solution)/shard_map/dot_general | solution.py:525
  532.7 46.5 %collective-permute-done.26 = bf16[352,1024]{1,0:T(8,128)(2,1)S(1)} collective-permute-done((bf16[352,1024]{1,0:T(8,128)(2,1)S(1)}, bf16[352,1024]{1,0:T(8,128)(2,1)S(1)}, u32[]{:S(2)}, u32[]{:S(2)}) %collective-permute-start.26) | collective-permute-done | bytes 720928 | tf_op jit(solution)/shard_map/ppermute | solution.py:562
  580.4 14.3 %collective-permute-done.25 = bf16[256,1408]{1,0:T(8,128)(2,1)S(1)} collective-permute-done((bf16[256,1408]{1,0:T(8,128)(2,1)S(1)}, bf16[256,1408]{1,0:T(8,128)(2,1)S(1)}, u32[]{:S(2)}, u32[]{:S(2)}) %collective-permute-start.25) | collective-permute-done | bytes 720928 | tf_op jit(solution)/shard_map/ppermute | solution.py:562
  595.7 12.1 %collective-permute-done.23 = bf16[256,1408]{1,0:T(8,128)(2,1)S(1)} collective-permute-done((bf16[256,1408]{1,0:T(8,128)(2,1)S(1)}, bf16[256,1408]{1,0:T(8,128)(2,1)S(1)}, u32[]{:S(2)}, u32[]{:S(2)}) %collective-permute-start.23) | collective-permute-done | bytes 720928 | tf_op jit(solution)/shard_map/ppermute | solution.py:562
  613.0 7.1 fusion.21
  637.8 10.6 convolution_convert_fusion.3.dmix_ref
  651.8 112.8 %mixer_backward.1 = (bf16[3072,3072]{1,0:T(8,128)(2,1)}, f32[3072,16]{1,0:T(8,128)}, f32[8,3072]{1,0:T(8,128)}, f32[4,8,2048]{2,1,0:T(8,128)}, f32[8,256]{1,0:T(8,128)}) custom-call(bf16[3072,1024]{1,0:T(8,128)(2,1)} %convolution_convert_fusion.3.dmix_ref, f32[3072,3072]{1,0:T(8,128)} %get-tuple-element.277.prev_ref.proj_ref, ...), custom_call_target="tpu_custom_call" | custom-call | flops 122880000000 | bytes 100663296 | tf_op jit(solution)/shard_map/mixer_backward/pallas_call | solution.py:401
  764.7 6.2 fusion.86
  785.9 14.7 %fusion.3 = f32[1536,1024]{1,0:T(8,128)S(1)} fusion(bf16[1024,3072]{1,0:T(8,128)(2,1)} %mix_ref.11, bf16[3072,3072]{1,0:T(8,128)(2,1)} %get-tuple-element.302, s32[]{:T(128)S(6)} %select_n.354), kind=kOutput, calls=%fused_computation.12 | convolution fusion | flops 9663676416 | bytes 22020100 | tf_op jit(solution)/shard_map/dot_general | solution.py:529
  800.7 5.6 fusion.7
  806.3 25.6 %convolution_convert_fusion.2 = bf16[1024,3072]{1,0:T(8,128)(2,1)S(1)} fusion(bf16[3072,1024]{1,0:T(8,128)(2,1)} %get-tuple-element.297, bf16[3072,3072]{1,0:T(8,128)(2,1)} %get-tuple-element.302), kind=kOutput, calls=%fused_computation.48 | convolution fusion | flops 19330498560 | bytes 31457280 | tf_op jit(solution)/shard_map/dot_general | solution.py:519
  844.5 6.1 collective-permute-done.33
  854.4 11.5 %collective-permute-done.32 = bf16[352,1024]{1,0:T(8,128)(2,1)S(1)} collective-permute-done((bf16[352,1024]{1,0:T(8,128)(2,1)S(1)}, bf16[352,1024]{1,0:T(8,128)(2,1)S(1)}, u32[]{:S(2)}, u32[]{:S(2)}) %collective-permute-start.32) | collective-permute-done | bytes 720928 | tf_op jit(solution)/shard_map/ppermute | solution.py:568
  866.2 15.3 %collective-permute-done.31 = bf16[256,1408]{1,0:T(8,128)(2,1)} collective-permute-done((bf16[256,1408]{1,0:T(8,128)(2,1)}, bf16[256,1408]{1,0:T(8,128)(2,1)}, u32[]{:S(2)}, u32[]{:S(2)}) %collective-permute-start.31) | collective-permute-done | bytes 720928 | tf_op jit(solution)/shard_map/ppermute | solution.py:568
  884.2 12.4 %collective-permute-done.30 = bf16[256,1408]{1,0:T(8,128)(2,1)} collective-permute-done((bf16[256,1408]{1,0:T(8,128)(2,1)}, bf16[256,1408]{1,0:T(8,128)(2,1)}, u32[]{:S(2)}, u32[]{:S(2)}) %collective-permute-start.30) | collective-permute-done | bytes 720928 | tf_op jit(solution)/shard_map/ppermute | solution.py:568
  899.2 4.7 add_convert_fusion
  905.2 4.5 fusion.55
  933.6 20.9 %fusion.16 = (f32[1024]{0:T(1024)S(1)}, f32[1536]{0:T(1024)S(1)}, f32[1536,1024]{1,0:T(8,128)}) fusion(bf16[1536,1024]{1,0:T(8,128)(2,1)} %param.19, f32[1536]{0:T(1024)S(1)} %copy-done.51, bf16[1536,1024]{1,0:T(8,128)(2,1)} %collective-permute-done.34, f32[1024]{0:T(1024)S(1)} %copy-done.43, f32[1536,1024]{1,0:T(8,128)} %fusion.55, ...), kind=kOutput, calls=%fused_computation.29 | convolution fusion | flops 9679403008 | bytes 34623492 | tf_op jit(solution)/shard_map/dot_general | solution.py:529
  962.8 5.2 collective-permute-done.41
  970.1 9.3 fusion.13
  984.4 60.5 %all-reduce.15.cloned.1.call-done = bf16[512,3072]{1,0:T(8,128)(2,1)} async-done(((bf16[512,3072]{1,0:T(8,128)(2,1)}), bf16[512,3072]{1,0:T(8,128)(2,1)}) %all-reduce.15.cloned.1.call-update) | async-done | bytes 3145744 | tf_op jit(solution)/shard_map/psum | solution.py:594
  1044.9 5.9 collective-permute-done.44
  1053.0 6.0 maximum_convert_fusion
  (407 shorter events, 224.1 us)
Async XLA Ops:
  7.2 62.2 %copy-start = (bf16[1024,1024]{1,0:T(8,128)(2,1)S(1)}, bf16[1024,1024]{1,0:T(8,128)(2,1)}, u32[]{:S(2)}) copy-start(bf16[1024,1024]{1,0:T(8,128)(2,1)} %param.28) | copy-start | bytes 6291460
  7.2 757.4 %all-reduce.17.cloned.1.call-start = ((), (), s32[]{:S(2)}) async-start(), calls=%async_computation.1 | async-start | bytes 5373952 | tf_op jit(solution)/shard_map/psum | solution.py:594
  11.0 26.3 %collective-permute-start = (bf16[512,1024]{1,0:T(8,128)(2,1)}, bf16[512,1024]{1,0:T(8,128)(2,1)S(1)}, u32[]{:S(2)}, u32[]{:S(2)}) collective-permute-start(bf16[512,1024]{1,0:T(8,128)(2,1)} %get-tuple-element.357.own_ref), channel_id=1, source_target_pairs={{0,1},{1,0},{2,3},{3,2},{4,5},{5,4},{6,7},{7,6},{8,9},{9,8},{10,11... | collective-permute-start | bytes 3145736 | tf_op jit(solution)/shard_map/ppermute | solution.py:562
  38.3 33.6 %collective-permute-start.1 = (bf16[512,1024]{1,0:T(8,128)(2,1)}, bf16[512,1024]{1,0:T(8,128)(2,1)S(1)}, u32[]{:S(2)}, u32[]{:S(2)}) collective-permute-start(bf16[512,1024]{1,0:T(8,128)(2,1)} %get-tuple-element.186.own_ref), channel_id=1, source_target_pairs={{0,1},{1,0},{2,3},{3,2},{4,5},{5,4},{6,7},{7,6},{8,9},{9,8},{10,11... | collective-permute-start | bytes 3145736 | tf_op jit(solution)/shard_map/ppermute | solution.py:562
  71.9 27.8 %collective-permute-start.2 = (bf16[512,1024]{1,0:T(8,128)(2,1)}, bf16[512,1024]{1,0:T(8,128)(2,1)}, u32[]{:S(2)}, u32[]{:S(2)}) collective-permute-start(bf16[512,1024]{1,0:T(8,128)(2,1)} %get-tuple-element.187.own_ref), channel_id=1, source_target_pairs={{0,1},{1,0},{2,3},{3,2},{4,5},{5,4},{6,7},{7,6},{8,9},{9,8},{10,11... | collective-permute-start | bytes 3145736 | tf_op jit(solution)/shard_map/ppermute | solution.py:562
  101.9 56.7 %collective-permute-start.4 = (bf16[256,1408]{1,0:T(8,128)(2,1)}, bf16[256,1408]{1,0:T(8,128)(2,1)S(1)}, u32[]{:S(2)}, u32[]{:S(2)}) collective-permute-start(bf16[256,1408]{1,0:T(8,128)(2,1)} %constant_dynamic-slice_fusion.13), channel_id=1, source_target_pairs={{0,1},{1,0},{2,3},{3,2},{4,5},{5,4},{6,7},{7,6},{8,9},{9,8},{10,11... | collective-permute-start | bytes 2162696 | tf_op jit(solution)/shard_map/ppermute | solution.py:562
  105.1 53.4 %collective-permute-start.5 = (bf16[256,1408]{1,0:T(8,128)(2,1)}, bf16[256,1408]{1,0:T(8,128)(2,1)S(1)}, u32[]{:S(2)}, u32[]{:S(2)}) collective-permute-start(bf16[256,1408]{1,0:T(8,128)(2,1)} %constant_dynamic-slice_fusion.12), channel_id=1, source_target_pairs={{0,1},{1,0},{2,3},{3,2},{4,5},{5,4},{6,7},{7,6},{8,9},{9,8},{10,11... | collective-permute-start | bytes 2162696 | tf_op jit(solution)/shard_map/ppermute | solution.py:562
  108.2 50.4 %collective-permute-start.6 = (bf16[352,1024]{1,0:T(8,128)(2,1)}, bf16[352,1024]{1,0:T(8,128)(2,1)}, u32[]{:S(2)}, u32[]{:S(2)}) collective-permute-start(bf16[352,1024]{1,0:T(8,128)(2,1)} %constant_dynamic-slice_fusion.11), channel_id=1, source_target_pairs={{0,1},{1,0},{2,3},{3,2},{4,5},{5,4},{6,7},{7,6},{8,9},{9,8},{10,11... | collective-permute-start | bytes 2162696 | tf_op jit(solution)/shard_map/ppermute | solution.py:562
  158.6 52.5 %collective-permute-start.11 = (bf16[352,1024]{1,0:T(8,128)(2,1)}, bf16[352,1024]{1,0:T(8,128)(2,1)}, u32[]{:S(2)}, u32[]{:S(2)}) collective-permute-start(bf16[352,1024]{1,0:T(8,128)(2,1)} %collective-permute-done.6), channel_id=1, source_target_pairs={{0,4},{2,6},{4,0},{6,2},{8,12},{10,14},{12,8},{14,10},{16,20},{18,... | collective-permute-start | bytes 2162696 | tf_op jit(solution)/shard_map/ppermute | solution.py:568
  160.1 52.5 %collective-permute-start.10 = (bf16[256,1408]{1,0:T(8,128)(2,1)S(1)}, bf16[256,1408]{1,0:T(8,128)(2,1)}, u32[]{:S(2)}, u32[]{:S(2)}) collective-permute-start(bf16[256,1408]{1,0:T(8,128)(2,1)S(1)} %collective-permute-done.5), channel_id=1, source_target_pairs={{0,4},{2,6},{4,0},{6,2},{8,12},{10,14},{12,8},{14,10},{16,20},{18,... | collective-permute-start | bytes 2162696 | tf_op jit(solution)/shard_map/ppermute | solution.py:568
  160.7 53.4 %collective-permute-start.9 = (bf16[256,1408]{1,0:T(8,128)(2,1)S(1)}, bf16[256,1408]{1,0:T(8,128)(2,1)}, u32[]{:S(2)}, u32[]{:S(2)}) collective-permute-start(bf16[256,1408]{1,0:T(8,128)(2,1)S(1)} %collective-permute-done.4), channel_id=1, source_target_pairs={{0,4},{2,6},{4,0},{6,2},{8,12},{10,14},{12,8},{14,10},{16,20},{18,... | collective-permute-start | bytes 2162696 | tf_op jit(solution)/shard_map/ppermute | solution.py:568
  215.5 12.5 %collective-permute-start.14 = (bf16[704,1024]{1,0:T(8,128)(2,1)S(1)}, bf16[704,1024]{1,0:T(8,128)(2,1)S(1)}, u32[]{:S(2)}, u32[]{:S(2)}) collective-permute-start(bf16[704,1024]{1,0:T(8,128)(2,1)S(1)} %pad_maximum_fusion.9), channel_id=1, source_target_pairs={{0,2},{2,0},{4,6},{6,4},{8,10},{10,8},{12,14},{14,12},{16,18},{18,... | collective-permute-start | bytes 4325384 | tf_op jit(solution)/shard_map/ppermute | solution.py:565
  218.6 42.8 %collective-permute-start.3 = (bf16[512,1024]{1,0:T(8,128)(2,1)}, bf16[512,1024]{1,0:T(8,128)(2,1)}, u32[]{:S(2)}, u32[]{:S(2)}) collective-permute-start(bf16[512,1024]{1,0:T(8,128)(2,1)} %get-tuple-element.416), channel_id=1, source_target_pairs={{0,1},{1,0},{2,3},{3,2},{4,5},{5,4},{6,7},{7,6},{8,9},{9,8},{10,11... | collective-permute-start | bytes 3145736 | tf_op jit(solution)/shard_map/ppermute | solution.py:562
  219.5 10.8 %collective-permute-start.13 = (bf16[512,1408]{1,0:T(8,128)(2,1)S(1)}, bf16[512,1408]{1,0:T(8,128)(2,1)S(1)}, u32[]{:S(2)}, u32[]{:S(2)}) collective-permute-start(bf16[512,1408]{1,0:T(8,128)(2,1)S(1)} %pad_maximum_fusion.8), channel_id=1, source_target_pairs={{0,2},{2,0},{4,6},{6,4},{8,10},{10,8},{12,14},{14,12},{16,18},{18,... | collective-permute-start | bytes 4325384 | tf_op jit(solution)/shard_map/ppermute | solution.py:565
  223.9 43.4 %collective-permute-start.8 = (bf16[512,1024]{1,0:T(8,128)(2,1)}, bf16[512,1024]{1,0:T(8,128)(2,1)}, u32[]{:S(2)}, u32[]{:S(2)}) collective-permute-start(bf16[512,1024]{1,0:T(8,128)(2,1)} %get-tuple-element.420), channel_id=1, source_target_pairs={{0,1},{1,0},{2,3},{3,2},{4,5},{5,4},{6,7},{7,6},{8,9},{9,8},{10,11... | collective-permute-start | bytes 3145736 | tf_op jit(solution)/shard_map/ppermute | solution.py:562
  225.1 7.0 collective-permute-start.12
  228.1 61.3 %collective-permute-start.7 = (bf16[512,1024]{1,0:T(8,128)(2,1)}, bf16[512,1024]{1,0:T(8,128)(2,1)}, u32[]{:S(2)}, u32[]{:S(2)}) collective-permute-start(bf16[512,1024]{1,0:T(8,128)(2,1)} %get-tuple-element.418), channel_id=1, source_target_pairs={{0,1},{1,0},{2,3},{3,2},{4,5},{5,4},{6,7},{7,6},{8,9},{9,8},{10,11... | collective-permute-start | bytes 3145736 | tf_op jit(solution)/shard_map/ppermute | solution.py:562
  378.8 66.5 %collective-permute-start.20 = (bf16[512,2816]{1,0:T(8,128)(2,1)}, bf16[512,2816]{1,0:T(8,128)(2,1)S(1)}, u32[]{:S(2)}, u32[]{:S(2)}) collective-permute-start(bf16[512,2816]{1,0:T(8,128)(2,1)} %constant_dynamic-slice_fusion.5), channel_id=1, source_target_pairs={{0,2},{2,0},{4,6},{6,4},{8,10},{10,8},{12,14},{14,12},{16,18},{18,... | collective-permute-start | bytes 8650760 | tf_op jit(solution)/shard_map/ppermute | solution.py:565
  392.9 16.9 %collective-permute-start.17 = (bf16[704,1024]{1,0:T(8,128)(2,1)S(1)}, bf16[704,1024]{1,0:T(8,128)(2,1)}, u32[]{:S(2)}, u32[]{:S(2)}) collective-permute-start(bf16[704,1024]{1,0:T(8,128)(2,1)S(1)} %constant_dynamic-slice_fusion.8), channel_id=1, source_target_pairs={{0,2},{2,0},{4,6},{6,4},{8,10},{10,8},{12,14},{14,12},{16,18},{18,... | collective-permute-start | bytes 4325384 | tf_op jit(solution)/shard_map/ppermute | solution.py:565
  393.1 19.4 %collective-permute-start.15 = (bf16[704,1024]{1,0:T(8,128)(2,1)S(1)}, bf16[704,1024]{1,0:T(8,128)(2,1)S(1)}, u32[]{:S(2)}, u32[]{:S(2)}) collective-permute-start(bf16[704,1024]{1,0:T(8,128)(2,1)S(1)} %constant_dynamic-slice_fusion.10), channel_id=1, source_target_pairs={{0,2},{2,0},{4,6},{6,4},{8,10},{10,8},{12,14},{14,12},{16,18},{18,... | collective-permute-start | bytes 4325384 | tf_op jit(solution)/shard_map/ppermute | solution.py:565
  407.7 38.4 %collective-permute-start.19 = (bf16[512,2816]{1,0:T(8,128)(2,1)S(1)}, bf16[512,2816]{1,0:T(8,128)(2,1)}, u32[]{:S(2)}, u32[]{:S(2)}) collective-permute-start(bf16[512,2816]{1,0:T(8,128)(2,1)S(1)} %constant_dynamic-slice_fusion.6), channel_id=1, source_target_pairs={{0,2},{2,0},{4,6},{6,4},{8,10},{10,8},{12,14},{14,12},{16,18},{18,... | collective-permute-start | bytes 8650760 | tf_op jit(solution)/shard_map/ppermute | solution.py:565
  411.8 19.1 %collective-permute-start.18 = (bf16[352,1024]{1,0:T(8,128)(2,1)S(1)}, bf16[352,1024]{1,0:T(8,128)(2,1)S(1)}, u32[]{:S(2)}, u32[]{:S(2)}) collective-permute-start(bf16[352,1024]{1,0:T(8,128)(2,1)S(1)} %constant_dynamic-slice_fusion.7), channel_id=1, source_target_pairs={{0,4},{2,6},{4,0},{6,2},{8,12},{10,14},{12,8},{14,10},{16,20},{18,... | collective-permute-start | bytes 2162696 | tf_op jit(solution)/shard_map/ppermute | solution.py:568
  413.2 31.9 %collective-permute-start.16 = (bf16[352,1024]{1,0:T(8,128)(2,1)S(1)}, bf16[352,1024]{1,0:T(8,128)(2,1)S(1)}, u32[]{:S(2)}, u32[]{:S(2)}) collective-permute-start(bf16[352,1024]{1,0:T(8,128)(2,1)S(1)} %constant_dynamic-slice_fusion.9), channel_id=1, source_target_pairs={{0,4},{2,6},{4,0},{6,2},{8,12},{10,14},{12,8},{14,10},{16,20},{18,... | collective-permute-start | bytes 2162696 | tf_op jit(solution)/shard_map/ppermute | solution.py:568
  451.4 43.4 %collective-permute-start.24 = (bf16[256,2816]{1,0:T(8,128)(2,1)}, bf16[256,2816]{1,0:T(8,128)(2,1)}, u32[]{:S(2)}, u32[]{:S(2)}) collective-permute-start(bf16[256,2816]{1,0:T(8,128)(2,1)} %constant_dynamic-slice_fusion.3), channel_id=1, source_target_pairs={{0,4},{2,6},{4,0},{6,2},{8,12},{10,14},{12,8},{14,10},{16,20},{18,... | collective-permute-start | bytes 4325384 | tf_op jit(solution)/shard_map/ppermute | solution.py:568
  453.4 61.5 %collective-permute-start.22 = (bf16[256,2816]{1,0:T(8,128)(2,1)}, bf16[256,2816]{1,0:T(8,128)(2,1)}, u32[]{:S(2)}, u32[]{:S(2)}) collective-permute-start(bf16[256,2816]{1,0:T(8,128)(2,1)} %constant_dynamic-slice_fusion.4), channel_id=1, source_target_pairs={{0,4},{2,6},{4,0},{6,2},{8,12},{10,14},{12,8},{14,10},{16,20},{18,... | collective-permute-start | bytes 4325384 | tf_op jit(solution)/shard_map/ppermute | solution.py:568
  492.8 116.0 %collective-permute-start.21 = (bf16[1536,1024]{1,0:T(8,128)(2,1)S(1)}, bf16[1536,1024]{1,0:T(8,128)(2,1)S(1)}, u32[]{:S(2)}, u32[]{:S(2)}) collective-permute-start(bf16[1536,1024]{1,0:T(8,128)(2,1)S(1)} %get-tuple-element.270), channel_id=1, source_target_pairs={{0,1},{1,0},{2,3},{3,2},{4,5},{5,4},{6,7},{7,6},{8,9},{9,8},{10,11... | collective-permute-start | bytes 9437192 | tf_op jit(solution)/shard_map/ppermute | solution.py:562
  494.3 85.0 %collective-permute-start.26 = (bf16[352,1024]{1,0:T(8,128)(2,1)S(1)}, bf16[352,1024]{1,0:T(8,128)(2,1)S(1)}, u32[]{:S(2)}, u32[]{:S(2)}) collective-permute-start(bf16[352,1024]{1,0:T(8,128)(2,1)S(1)} %add_convert_fusion.10), channel_id=1, source_target_pairs={{0,1},{1,0},{2,3},{3,2},{4,5},{5,4},{6,7},{7,6},{8,9},{9,8},{10,11... | collective-permute-start | bytes 2162696 | tf_op jit(solution)/shard_map/ppermute | solution.py:562
  496.6 98.1 %collective-permute-start.25 = (bf16[256,1408]{1,0:T(8,128)(2,1)S(1)}, bf16[256,1408]{1,0:T(8,128)(2,1)S(1)}, u32[]{:S(2)}, u32[]{:S(2)}) collective-permute-start(bf16[256,1408]{1,0:T(8,128)(2,1)S(1)} %slice.204), channel_id=1, source_target_pairs={{0,1},{1,0},{2,3},{3,2},{4,5},{5,4},{6,7},{7,6},{8,9},{9,8},{10,11... | collective-permute-start | bytes 2162696 | tf_op jit(solution)/shard_map/ppermute | solution.py:562
  516.7 91.1 %collective-permute-start.23 = (bf16[256,1408]{1,0:T(8,128)(2,1)S(1)}, bf16[256,1408]{1,0:T(8,128)(2,1)S(1)}, u32[]{:S(2)}, u32[]{:S(2)}) collective-permute-start(bf16[256,1408]{1,0:T(8,128)(2,1)S(1)} %slice.202), channel_id=1, source_target_pairs={{0,1},{1,0},{2,3},{3,2},{4,5},{5,4},{6,7},{7,6},{8,9},{9,8},{10,11... | collective-permute-start | bytes 2162696 | tf_op jit(solution)/shard_map/ppermute | solution.py:562
  620.2 14.3 %collective-permute-start.27 = (bf16[512,1024]{1,0:T(8,128)(2,1)S(1)}, bf16[512,1024]{1,0:T(8,128)(2,1)}, u32[]{:S(2)}, u32[]{:S(2)}) collective-permute-start(bf16[512,1024]{1,0:T(8,128)(2,1)S(1)} %constant_dynamic-slice_fusion.2), channel_id=1, source_target_pairs={{0,2},{2,0},{4,6},{6,4},{8,10},{10,8},{12,14},{14,12},{16,18},{18,... | collective-permute-start | bytes 3145736 | tf_op jit(solution)/shard_map/ppermute | solution.py:565
  636.7 14.0 %collective-permute-start.28 = (bf16[256,1024]{1,0:T(8,128)(2,1)S(1)}, bf16[256,1024]{1,0:T(8,128)(2,1)S(1)}, u32[]{:S(2)}, u32[]{:S(2)}) collective-permute-start(bf16[256,1024]{1,0:T(8,128)(2,1)S(1)} %constant_dynamic-slice_fusion.1), channel_id=1, source_target_pairs={{0,4},{2,6},{4,0},{6,2},{8,12},{10,14},{12,8},{14,10},{16,20},{18,... | collective-permute-start | bytes 1572872 | tf_op jit(solution)/shard_map/ppermute | solution.py:568
  651.7 393.1 %all-reduce.15.cloned.1.call-start = ((), (), s32[]{:S(2)}) async-start(), calls=%async_computation | async-start | bytes 6291456 | tf_op jit(solution)/shard_map/psum | solution.py:594
  835.5 63.7 %collective-permute-start.29 = (bf16[512,3072]{1,0:T(8,128)(2,1)}, bf16[512,3072]{1,0:T(8,128)(2,1)}, u32[]{:S(2)}, u32[]{:S(2)}) collective-permute-start(bf16[512,3072]{1,0:T(8,128)(2,1)} %constant_dynamic-slice_fusion), channel_id=1, source_target_pairs={{0,2},{2,0},{4,6},{6,4},{8,10},{10,8},{12,14},{14,12},{16,18},{18,... | collective-permute-start | bytes 9437192 | tf_op jit(solution)/shard_map/ppermute | solution.py:565
  835.6 15.0 %collective-permute-start.33 = (bf16[256,1024]{1,0:T(8,128)(2,1)}, bf16[256,1024]{1,0:T(8,128)(2,1)}, u32[]{:S(2)}, u32[]{:S(2)}) collective-permute-start(bf16[256,1024]{1,0:T(8,128)(2,1)} %get-tuple-element.301), channel_id=1, source_target_pairs={{0,4},{2,6},{4,0},{6,2},{8,12},{10,14},{12,8},{14,10},{16,20},{18,... | collective-permute-start | bytes 1572872 | tf_op jit(solution)/shard_map/ppermute | solution.py:568
  836.5 29.4 %collective-permute-start.32 = (bf16[352,1024]{1,0:T(8,128)(2,1)S(1)}, bf16[352,1024]{1,0:T(8,128)(2,1)S(1)}, u32[]{:S(2)}, u32[]{:S(2)}) collective-permute-start(bf16[352,1024]{1,0:T(8,128)(2,1)S(1)} %copy-done.40), channel_id=1, source_target_pairs={{0,4},{2,6},{4,0},{6,2},{8,12},{10,14},{12,8},{14,10},{16,20},{18,... | collective-permute-start | bytes 2162696 | tf_op jit(solution)/shard_map/ppermute | solution.py:568
  839.5 42.0 %collective-permute-start.31 = (bf16[256,1408]{1,0:T(8,128)(2,1)}, bf16[256,1408]{1,0:T(8,128)(2,1)}, u32[]{:S(2)}, u32[]{:S(2)}) collective-permute-start(bf16[256,1408]{1,0:T(8,128)(2,1)} %get-tuple-element.299), channel_id=1, source_target_pairs={{0,4},{2,6},{4,0},{6,2},{8,12},{10,14},{12,8},{14,10},{16,20},{18,... | collective-permute-start | bytes 2162696 | tf_op jit(solution)/shard_map/ppermute | solution.py:568
  840.4 56.1 %collective-permute-start.30 = (bf16[256,1408]{1,0:T(8,128)(2,1)}, bf16[256,1408]{1,0:T(8,128)(2,1)}, u32[]{:S(2)}, u32[]{:S(2)}) collective-permute-start(bf16[256,1408]{1,0:T(8,128)(2,1)} %get-tuple-element.298), channel_id=1, source_target_pairs={{0,4},{2,6},{4,0},{6,2},{8,12},{10,14},{12,8},{14,10},{16,20},{18,... | collective-permute-start | bytes 2162696 | tf_op jit(solution)/shard_map/ppermute | solution.py:568
  850.6 82.9 %collective-permute-start.34 = (bf16[1536,1024]{1,0:T(8,128)(2,1)}, bf16[1536,1024]{1,0:T(8,128)(2,1)}, u32[]{:S(2)}, u32[]{:S(2)}) collective-permute-start(bf16[1536,1024]{1,0:T(8,128)(2,1)} %get-tuple-element.303), channel_id=1, source_target_pairs={{0,1},{1,0},{2,3},{3,2},{4,5},{5,4},{6,7},{7,6},{8,9},{9,8},{10,11... | collective-permute-start | bytes 9437192 | tf_op jit(solution)/shard_map/ppermute | solution.py:562
  904.0 10.6 collective-permute-start.38
  904.6 14.1 %collective-permute-start.37 = (bf16[704,1024]{1,0:T(8,128)(2,1)S(1)}, bf16[704,1024]{1,0:T(8,128)(2,1)}, u32[]{:S(2)}, u32[]{:S(2)}) collective-permute-start(bf16[704,1024]{1,0:T(8,128)(2,1)S(1)} %pad_maximum_fusion.12), channel_id=1, source_target_pairs={{0,2},{2,0},{4,6},{6,4},{8,10},{10,8},{12,14},{14,12},{16,18},{18,... | collective-permute-start | bytes 4325384 | tf_op jit(solution)/shard_map/ppermute | solution.py:565
  914.0 9.6 collective-permute-start.36
  914.1 14.4 %collective-permute-start.35 = (bf16[512,1408]{1,0:T(8,128)(2,1)}, bf16[512,1408]{1,0:T(8,128)(2,1)}, u32[]{:S(2)}, u32[]{:S(2)}) collective-permute-start(bf16[512,1408]{1,0:T(8,128)(2,1)} %pad_maximum_fusion.10), channel_id=1, source_target_pairs={{0,2},{2,0},{4,6},{6,4},{8,10},{10,8},{12,14},{14,12},{16,18},{18,... | collective-permute-start | bytes 4325384 | tf_op jit(solution)/shard_map/ppermute | solution.py:565
  954.8 1.4 collective-permute-start.39
  956.2 4.9 collective-permute-start.40
  961.1 6.9 collective-permute-start.41
  968.0 11.3 %collective-permute-start.42 = (f32[19,1024]{1,0:T(8,128)S(1)}, f32[19,1024]{1,0:T(8,128)S(1)}, u32[]{:S(2)}, u32[]{:S(2)}) collective-permute-start(f32[19,1024]{1,0:T(8,128)S(1)} %add.325), channel_id=1, source_target_pairs={{0,16},{2,18},{4,20},{6,22},{8,24},{10,26},{12,28},{14,30},{16,0},... | collective-permute-start | bytes 233480 | tf_op jit(solution)/shard_map/ppermute | solution.py:602
  979.4 3.8 collective-permute-start.43
  1044.9 5.9 collective-permute-start.44
  (82 other events, 668.6 us)
Sparse Core Ops, SparseCore 0:
  651.9 108.0 all-reduce.16
  914.7 130.1 all-reduce.14

commit v2 on v1

--- a/solution.py
+++ b/solution.py
@@ -671,6 +671,9 @@
         if p == cuts:
             fetched, state = tied(fetched, state)
             fetched = [move.join(f, move.along(f), move.side) for f in fetched]
+        if p > cuts:
+            now, attn_got[-1] = tied(now, attn_got[-1])
+            mixed[-1] = now
         if p >= cuts:
             low, high = wide_dot(mixed[p - cuts], out_weight), wide_dot(now, out_weight)
             attn_own.append(jnp.where(here == 0, low, high))
@@ -703,10 +706,10 @@
     down_halves = [move.halve(grad_down[:width]), move.halve(grad_down[width:])]
     gate_half = move.halve(cross(second_low, gate_grad).astype(LOW))
     up_half = move.halve(cross(second_low, up_grad).astype(LOW))
+    gate_in, up_in, down_halves, gate_half, up_half = tied(
+        gate_grad, up_grad, down_halves, gate_half, up_half
+    )
     down_mine, down_sent = [move.quarter(d) for d in down_halves]
-    gate_in, up_in, down_mine, down_sent, gate_half, up_half = tied(
-        gate_grad, up_grad, down_mine, down_sent, gate_half, up_half
-    )
     gate_half, up_half = move.quarter(gate_half), move.quarter(up_half)
     down_sent = move.across(down_sent)
     gate_sent = move.across(gate_half[:, width:])
@@ -721,9 +724,8 @@
     mixed = jnp.concatenate(mixed, axis=0)
     gate_sum = gate_half[:, :width] + gate_sent
     up_sum = up_half[:, :width] + up_sent
-    attn_sent, block_out, mixed, gate_sum, up_sum, down_sum = tied(
-        attn_sent, block_out, mixed, gate_sum, up_sum, down_mine + down_sent
-    )
+    down_sum = down_mine + down_sent
+    attn_sent, block_out, mixed = tied(attn_sent, block_out, mixed)
     attn_grad = move.join(attn_low, attn_sent, here)
     dmixed = back_dot(attn_grad, out_weight).astype(LOW)
     grad_out = move.quarter(move.halve(cross(mixed, attn_grad).astype(LOW)))
@@ -733,7 +735,6 @@
     back = mixer_bwd(dmixed, marks, line, conv_weight, out_gain[None], kept, 0, 1)
     back, sums_ffn = tied(back, sums_ffn)
     dproj = back[0]
-    sums_ffn = move.halves(sums_ffn)
     dprep, dtaps, dgain = merge_back([back], heads)
     rates_grad, grad_log, grad_bias = rates_back(
         kept[1], decay_log, decay_bias, segment, dprep
@@ -750,8 +751,9 @@
     dproj, theirs_low = tied(dproj, theirs_low)
     sent = move.across(theirs_low)
     half = move.halve(cross(first_rows, dproj).astype(LOW))
-    dproj, half, sums_ffn = tied(dproj, half, sums_ffn)
+    dproj, half = tied(dproj, half)
     (sum_mix,) = move.sum((half,), 1)
+    sums_ffn = move.halves(sums_ffn)
     mine = first_part(dproj, here)
     grad_rate = cross(rates_low, first_rows)
     token_own = inputs

time: 1080 us -> 1040 us (0.963)
  waiting for transfers between devices: 278 us -> 248 us
    ppermute x15, waiting for transfers between devices: 111 us -> 36.5 us  [across(): return lax.ppermute(value, 'tensor', [(0, 1), (1, 0)])]
    ppermute x12, waiting for transfers between devices: 90.1 us -> 112 us  [along(): return lax.ppermute(value, 'dp', self.sides)]
    psum x2, waiting for transfers between devices: 60.5 us -> 76.5 us  [sum(): return lax.psum(values, 'dp', axis_index_groups=orders)]
    unnamed x173 -> x193, local copies, waits for them, and re-layouts: 22.5 us -> 21.8 us
  transfers between devices with their start and end apart: 47 -> 47, of which waited for: 20 -> 18; matrix products, arithmetic and copies ran while one was open for 26% -> 24% of each run, Pallas kernels for 24% -> 25%
where the time goes in v2:
time: 1040 us; the launch traced here: 1030 us
  Pallas kernels  260 us (25%)
  matrix products  249 us (24%)
  waiting for transfers between devices  248 us (24%)
  other arithmetic  146 us (14%)
  local copies, waits for them, and re-layouts  79.2 us (8%)
  starting transfers between devices  34 us (3%)
  between operations  16 us (2%)
    pallas_call x6, Pallas kernels, mixer_fwd(): pl.pallas_call(fwd_kernel, grid=(x.shape[0] // CHUNK,), in_specs=in_specs...  147 us
    pallas_call x1, Pallas kernels, mixer_bwd(): pl.pallas_call(partial(bwd_kernel, first=group * heads, total_heads=whole...  113 us
    ppermute x12, waiting for transfers between devices, along(): return lax.ppermute(value, 'dp', self.sides)  112 us
    dot_general x8, matrix products, back_dot(): lax.dot_general(grad, weight, (((1,), (1,)), ((), ())), preferred_element...  103 us
    psum x2, waiting for transfers between devices, sum(): return lax.psum(values, 'dp', axis_index_groups=orders)  76.5 us
    dot_general x9, matrix products, wide_dot(): return jnp.dot(left, right, preferred_element_type=F32)  74.2 us
    dot_general x6, matrix products, cross(): lax.dot_general(left, right, (((0,), (0,)), ((), ())), preferred_element_...  71.1 us
    ppermute x15, waiting for transfers between devices, across(): return lax.ppermute(value, 'tensor', [(0, 1), (1, 0)])  36.5 us
  transfers between devices with their start and end apart: 47, of which 18 were waited for; matrix products, arithmetic and copies ran while one was open for 24% of the time, Pallas kernels for 25%

profile of v2, /device:TPU:0, one launch (start us, length us, event | category | flops | bytes accessed | tf_op | source)
XLA Modules:
  0.0 1032.7 jit_solution(11835744796401044280)
XLA Ops:
  27.9 9.4 collective-permute-done.got_ref
  42.9 24.2 %mixer_forward.6 = (bf16[512,1024]{1,0:T(8,128)(2,1)}, bf16[3072,1024]{1,0:T(8,128)(2,1)}, f32[3072,3072]{1,0:T(8,128)}, f32[3072,128]{1,0:T(8,128)}, f32[8,3072...) custom-call(f32[1,1]{1,0:T(1,128)} %bitcast.2.pick_ref, ...), custom_call_target="tpu_custom_call" | custom-call | flops 20480000000 | bytes 16777216 | tf_op jit(solution)/shard_map/mixer_forward/pallas_call | solution.py:368
  70.7 24.3 %mixer_forward.7 = (bf16[512,1024]{1,0:T(8,128)(2,1)}, bf16[3072,1024]{1,0:T(8,128)(2,1)}, f32[3072,3072]{1,0:T(8,128)}, f32[3072,128]{1,0:T(8,128)}, f32[8,3072...) custom-call(f32[1,1]{1,0:T(1,128)} %bitcast.2.pick_ref, ...), custom_call_target="tpu_custom_call", output_to_operand_aliasing={{1}: (13, {}), {2}: (14, {}), {3}: (15, {}), {4}: (16, {}),... | custom-call | flops 20480000000 | bytes 16777216 | tf_op jit(solution)/shard_map/mixer_forward/pallas_call | solution.py:368
  106.3 24.5 %mixer_forward.8 = (bf16[512,1024]{1,0:T(8,128)(2,1)}, bf16[3072,1024]{1,0:T(8,128)(2,1)}, f32[3072,3072]{1,0:T(8,128)}, f32[3072,128]{1,0:T(8,128)}, f32[8,3072...) custom-call(f32[1,1]{1,0:T(1,128)} %bitcast.2.pick_ref, ...), custom_call_target="tpu_custom_call", output_to_operand_aliasing={{1}: (13, {}), {2}: (14, {}), {3}: (15, {}), {4}: (16, {}),... | custom-call | flops 20480000000 | bytes 16777216 | tf_op jit(solution)/shard_map/mixer_forward/pallas_call | solution.py:368
  130.8 24.4 %mixer_forward.9 = (bf16[512,1024]{1,0:T(8,128)(2,1)}, bf16[3072,1024]{1,0:T(8,128)(2,1)}, f32[3072,3072]{1,0:T(8,128)}, f32[3072,128]{1,0:T(8,128)}, f32[8,3072...) custom-call(f32[1,1]{1,0:T(1,128)S(6)} %sub.60.pick_ref, ...), custom_call_target="tpu_custom_call", output_to_operand_aliasing={{1}: (13, {}), {2}: (14, {}), {3}: (15, {}), {4}: (16, {}),... | custom-call | flops 20480000000 | bytes 16777216 | tf_op jit(solution)/shard_map/mixer_forward/pallas_call | solution.py:368
  155.3 4.2 select_convert_fusion.2
  164.0 24.6 %mixer_forward.10 = (bf16[512,1024]{1,0:T(8,128)(2,1)}, bf16[3072,1024]{1,0:T(8,128)(2,1)}, f32[3072,3072]{1,0:T(8,128)}, f32[3072,128]{1,0:T(8,128)}, f32[8,307...) custom-call(f32[1,1]{1,0:T(1,128)S(6)} %sub.60.pick_ref, ...), custom_call_target="tpu_custom_call", output_to_operand_aliasing={{1}: (13, {}), {2}: (14, {}), {3}: (15, {}), {4}: (16, {}),... | custom-call | flops 20480000000 | bytes 16777216 | tf_op jit(solution)/shard_map/mixer_forward/pallas_call | solution.py:368
  188.5 24.5 %mixer_forward.11 = (bf16[512,1024]{1,0:T(8,128)(2,1)}, bf16[3072,1024]{1,0:T(8,128)(2,1)}, f32[3072,3072]{1,0:T(8,128)}, f32[3072,128]{1,0:T(8,128)}, f32[8,307...) custom-call(f32[1,1]{1,0:T(1,128)S(6)} %sub.60.pick_ref, ...), custom_call_target="tpu_custom_call", output_to_operand_aliasing={{1}: (13, {}), {2}: (14, {}), {3}: (15, {}), {4}: (16, {}),... | custom-call | flops 20480000000 | bytes 16777216 | tf_op jit(solution)/shard_map/mixer_forward/pallas_call | solution.py:368
  221.4 16.0 %collective-permute-done.7 = bf16[512,1024]{1,0:T(8,128)(2,1)S(1)} collective-permute-done((bf16[512,1024]{1,0:T(8,128)(2,1)S(1)}, bf16[512,1024]{1,0:T(8,128)(2,1)S(1)}, u32[]{:S(2)}, u32[]{:S(2)}) %collective-permute-start.7) | collective-permute-done | bytes 1048608 | tf_op jit(solution)/shard_map/ppermute | solution.py:562
  253.6 5.4 pad_maximum_fusion.1
  259.1 5.8 maximum_maximum_fusion.1
  264.8 16.1 %maximum_maximum_fusion = bf16[1024,2816]{1,0:T(8,128)(2,1)} fusion(bf16[512,1408]{1,0:T(8,128)(2,1)S(1)} %copy-done.27, bf16[512,1408]{1,0:T(8,128)(2,1)S(1)} %copy-done.26, bf16[1024,1408]{1,0:T(8,128)(2,1)} %param.30), kind=kLoop, calls=%fused_computation.41 | loop fusion | flops 17301504 | bytes 11534336 | tf_op jit(solution)/shard_map/concatenate | solution.py:683
  296.0 11.9 %fusion.95 = f32[1536,2816]{1,0:T(8,128)} fusion(bf16[1536,1024]{1,0:T(8,128)(2,1)S(1)} %multiply_convert_fusion.4, bf16[1024,2816]{1,0:T(8,128)(2,1)S(1)} %bitcast.148), kind=kOutput, calls=%fused_computation.260 | convolution fusion | flops 8858370048 | bytes 26214400 | tf_op jit(solution)/shard_map/dot_general | solution.py:525
  307.9 14.4 %fusion.32 = f32[1536,2816]{1,0:T(8,128)} fusion(bf16[2816,1024]{1,0:T(8,128)(2,1)S(1)} %bitcast.146, bf16[1536,1024]{1,0:T(8,128)(2,1)} %param.33, f32[1536]{0:T(1024)S(1)} %fusion.75), kind=kOutput, calls=%fused_computation.112 | convolution fusion | flops 8863088640 | bytes 26220544 | tf_op jit(solution)/shard_map/dot_general | solution.py:529
  322.4 31.7 %multiply_convert_fusion = (bf16[1536,2816]{1,0:T(8,128)(2,1)}, bf16[1536,2816]{1,0:T(8,128)(2,1)}, bf16[1536,2816]{1,0:T(8,128)(2,1)}) fusion(f32[1536,2816]{1,0:T(8,128)} %fusion.95, f32[1536,2816]{1,0:T(8,128)} %fusion.32, bf16[1536,1024]{1,0:T(8,128)(2,1)} %copy-done.31, bf16[1024,2816]{1,0:T(8,128)(2,1)} %maximum_maximum_fusion.1), kind=kOutput, calls=%fused_computation | convolution fusion | flops 8923250688 | bytes 69468160 | tf_op jit(solution)/shard_map/dot_general | solution.py:525
  354.1 13.7 %convolution_convert_fusion = bf16[1024,2816]{1,0:T(8,128)(2,1)S(1)} fusion(bf16[1536,1024]{1,0:T(8,128)(2,1)} %copy-done.31, bf16[1536,2816]{1,0:T(8,128)(2,1)} %get-tuple-element.263), kind=kOutput, calls=%fused_computation.46 | convolution fusion | flops 8861253632 | bytes 17563648 | tf_op jit(solution)/shard_map/dot_general | solution.py:519
  372.1 10.0 convolution_convert_fusion.1
  387.5 10.2 convolution_convert_fusion.4
  426.0 5.1 add_convert_fusion.2
  431.2 4.3 add_convert_fusion.3
  435.5 13.5 %fusion.96 = f32[1536,1024]{1,0:T(8,128)} fusion(bf16[1536,2816]{1,0:T(8,128)(2,1)} %get-tuple-element.263, bf16[1024,2816]{1,0:T(8,128)(2,1)S(1)} %bitcast.150), kind=kOutput, calls=%fused_computation.261 | convolution fusion | flops 8858370048 | bytes 20709376 | tf_op jit(solution)/shard_map/dot_general | solution.py:529
  449.0 17.5 %multiply_reduce_fusion = (f32[1024]{0:T(1024)}, f32[1536]{0:T(1024)S(1)}, f32[1536,1024]{1,0:T(8,128)}) fusion(f32[1536,1024]{1,0:T(8,128)S(1)} %bitcast.136, f32[1536]{0:T(1024)S(1)} %get-tuple-element.405, f32[1024]{0:T(1024)S(1)} %copy-done.61, f32[1536,1024]{1,0:T(8,128)} %fusion.96, bf16[1536,2816]{1,0:T(8,128)(2,1)} %get-tuple-element.262, ...), kind=kOutput, calls=%fused_computation.33 | convolution fusion | flops 8869378048 | bytes 33312768 | tf_op jit(solution)/shard_map/dot_general | solution.py:529
  466.5 6.8 multiply_convert_fusion.3
  479.3 14.6 %add_convert_fusion.1 = bf16[1536,1024]{1,0:T(8,128)(2,1)} fusion(f32[1536,1024]{1,0:T(8,128)S(1)} %bitcast.136, bf16[1536,2816]{1,0:T(8,128)(2,1)} %get-tuple-element.264, bf16[2816,1024]{1,0:T(8,128)(2,1)} %pad_maximum_fusion.1, f32[1536]{0:T(1024)S(1)} %fusion.75), kind=kOutput, calls=%fused_computation.36 | convolution fusion | flops 8863088640 | bytes 23861248 | tf_op jit(solution)/shard_map/dot_general | solution.py:525
  497.1 28.2 %collective-permute-done.22 = bf16[256,2816]{1,0:T(8,128)(2,1)} collective-permute-done((bf16[256,2816]{1,0:T(8,128)(2,1)S(1)}, bf16[256,2816]{1,0:T(8,128)(2,1)}, u32[]{:S(2)}, u32[]{:S(2)}) %collective-permute-start.22) | collective-permute-done | bytes 1441824 | tf_op jit(solution)/shard_map/ppermute | solution.py:568
  527.3 28.8 %collective-permute-done.20 = bf16[256,2816]{1,0:T(8,128)(2,1)S(1)} collective-permute-done((bf16[256,2816]{1,0:T(8,128)(2,1)}, bf16[256,2816]{1,0:T(8,128)(2,1)S(1)}, u32[]{:S(2)}, u32[]{:S(2)}) %collective-permute-start.20) | collective-permute-done | bytes 1441824 | tf_op jit(solution)/shard_map/ppermute | solution.py:568
  556.7 14.1 %collective-permute-done.24 = bf16[352,1024]{1,0:T(8,128)(2,1)S(1)} collective-permute-done((bf16[352,1024]{1,0:T(8,128)(2,1)S(1)}, bf16[352,1024]{1,0:T(8,128)(2,1)S(1)}, u32[]{:S(2)}, u32[]{:S(2)}) %collective-permute-start.24) | collective-permute-done | bytes 720928 | tf_op jit(solution)/shard_map/ppermute | solution.py:568
  572.5 8.8 fusion.21
  582.4 7.9 collective-permute-done.21
  592.3 11.4 %convolution_convert_fusion.3.dmix_ref = bf16[3072,1024]{1,0:T(8,128)(2,1)} fusion(bf16[1024,1024]{1,0:T(8,128)(2,1)S(1)} %copy-done, bf16[1536,1024]{1,0:T(8,128)(2,1)S(1)} %get-tuple-element.346, bf16[1536,1024]{1,0:T(8,128)(2,1)S(1)} %get-tuple-element.345), kind=kOutput, calls=%fused_computation.49 | convolution fusion | flops 6458179584 | bytes 14680064 | tf_op jit(solution)/shard_map/dot_general | solution.py:529
  606.5 113.2 %mixer_backward.1 = (bf16[3072,3072]{1,0:T(8,128)(2,1)}, f32[3072,16]{1,0:T(8,128)}, f32[8,3072]{1,0:T(8,128)}, f32[4,8,2048]{2,1,0:T(8,128)}, f32[8,256]{1,0:T(8,128)}) custom-call(bf16[3072,1024]{1,0:T(8,128)(2,1)} %convolution_convert_fusion.3.dmix_ref, f32[3072,3072]{1,0:T(8,128)} %get-tuple-element.275.prev_ref.proj_ref, ...), custom_call_target="tpu_custom_call" | custom-call | flops 122880000000 | bytes 100663296 | tf_op jit(solution)/shard_map/mixer_backward/pallas_call | solution.py:401
  719.7 6.1 fusion.87
  741.1 4.5 fusion.97
  745.6 14.7 %fusion.3 = f32[1536,1024]{1,0:T(8,128)S(1)} fusion(bf16[1024,3072]{1,0:T(8,128)(2,1)} %mix_ref.11, bf16[3072,3072]{1,0:T(8,128)(2,1)} %get-tuple-element.296, s32[]{:T(128)S(6)} %select_n.354), kind=kOutput, calls=%fused_computation.12 | convolution fusion | flops 9663676416 | bytes 22020100 | tf_op jit(solution)/shard_map/dot_general | solution.py:529
  760.3 5.6 fusion.7
  765.9 23.9 %convolution_convert_fusion.2 = bf16[1024,3072]{1,0:T(8,128)(2,1)S(1)} fusion(bf16[3072,1024]{1,0:T(8,128)(2,1)S(1)} %bitcast.134, bf16[3072,3072]{1,0:T(8,128)(2,1)} %get-tuple-element.296), kind=kOutput, calls=%fused_computation.48 | convolution fusion | flops 19330498560 | bytes 31457280 | tf_op jit(solution)/shard_map/dot_general | solution.py:519
  803.7 4.5 fusion.56
  811.6 12.4 %collective-permute-done.35 = bf16[352,1024]{1,0:T(8,128)(2,1)} collective-permute-done((bf16[352,1024]{1,0:T(8,128)(2,1)}, bf16[352,1024]{1,0:T(8,128)(2,1)}, u32[]{:S(2)}, u32[]{:S(2)}) %collective-permute-start.35) | collective-permute-done | bytes 720928 | tf_op jit(solution)/shard_map/ppermute | solution.py:568
  825.4 14.1 %collective-permute-done.33 = bf16[256,1408]{1,0:T(8,128)(2,1)} collective-permute-done((bf16[256,1408]{1,0:T(8,128)(2,1)S(1)}, bf16[256,1408]{1,0:T(8,128)(2,1)}, u32[]{:S(2)}, u32[]{:S(2)}) %collective-permute-start.33) | collective-permute-done | bytes 720928 | tf_op jit(solution)/shard_map/ppermute | solution.py:568
  840.8 12.0 %collective-permute-done.31 = bf16[256,1408]{1,0:T(8,128)(2,1)} collective-permute-done((bf16[256,1408]{1,0:T(8,128)(2,1)S(1)}, bf16[256,1408]{1,0:T(8,128)(2,1)}, u32[]{:S(2)}, u32[]{:S(2)}) %collective-permute-start.31) | collective-permute-done | bytes 720928 | tf_op jit(solution)/shard_map/ppermute | solution.py:568
  870.5 4.8 add_convert_fusion
  878.2 21.6 %fusion.16 = (f32[1024]{0:T(1024)S(1)}, f32[1536]{0:T(1024)S(1)}, f32[1536,1024]{1,0:T(8,128)}) fusion(bf16[1536,1024]{1,0:T(8,128)(2,1)} %param.19, f32[1536]{0:T(1024)S(1)} %copy-done.56, bf16[1536,1024]{1,0:T(8,128)(2,1)} %collective-permute-done.30, f32[1024]{0:T(1024)S(1)} %copy-done.47, f32[1536,1024]{1,0:T(8,128)} %fusion.56, ...), kind=kOutput, calls=%fused_computation.29 | convolution fusion | flops 9679403008 | bytes 34623492 | tf_op jit(solution)/shard_map/dot_general | solution.py:529
  901.6 4.8 collective-permute-done.40
  908.1 11.4 %collective-permute-done.41 = f32[19,1024]{1,0:T(8,128)S(1)} collective-permute-done((f32[19,1024]{1,0:T(8,128)S(1)}, f32[19,1024]{1,0:T(8,128)S(1)}, u32[]{:S(2)}, u32[]{:S(2)}) %collective-permute-start.41) | collective-permute-done | bytes 77856 | tf_op jit(solution)/shard_map/ppermute | solution.py:602
  920.5 9.3 fusion.13
  934.8 76.5 %all-reduce.15.cloned.1.call-done = bf16[512,3072]{1,0:T(8,128)(2,1)} async-done(((bf16[512,3072]{1,0:T(8,128)(2,1)}), bf16[512,3072]{1,0:T(8,128)(2,1)}) %all-reduce.15.cloned.1.call-update) | async-done | bytes 3145744 | tf_op jit(solution)/shard_map/psum | solution.py:594
  1011.3 5.9 collective-permute-done.44
  1019.4 6.0 maximum_convert_fusion
  (428 shorter events, 209.2 us)
Async XLA Ops:
  7.2 59.9 %copy-start = (bf16[1024,1024]{1,0:T(8,128)(2,1)S(1)}, bf16[1024,1024]{1,0:T(8,128)(2,1)}, u32[]{:S(2)}) copy-start(bf16[1024,1024]{1,0:T(8,128)(2,1)} %param.28) | copy-start | bytes 6291460
  7.2 712.5 %all-reduce.17.cloned.1.call-start = ((), (), s32[]{:S(2)}) async-start(), calls=%async_computation.1 | async-start | bytes 5373952 | tf_op jit(solution)/shard_map/psum | solution.py:594
  11.0 26.3 %collective-permute-start = (bf16[512,1024]{1,0:T(8,128)(2,1)}, bf16[512,1024]{1,0:T(8,128)(2,1)S(1)}, u32[]{:S(2)}, u32[]{:S(2)}) collective-permute-start(bf16[512,1024]{1,0:T(8,128)(2,1)} %get-tuple-element.351.own_ref), channel_id=1, source_target_pairs={{0,1},{1,0},{2,3},{3,2},{4,5},{5,4},{6,7},{7,6},{8,9},{9,8},{10,11... | collective-permute-start | bytes 3145736 | tf_op jit(solution)/shard_map/ppermute | solution.py:562
  38.3 31.3 %collective-permute-start.1 = (bf16[512,1024]{1,0:T(8,128)(2,1)}, bf16[512,1024]{1,0:T(8,128)(2,1)S(1)}, u32[]{:S(2)}, u32[]{:S(2)}) collective-permute-start(bf16[512,1024]{1,0:T(8,128)(2,1)} %get-tuple-element.183.own_ref), channel_id=1, source_target_pairs={{0,1},{1,0},{2,3},{3,2},{4,5},{5,4},{6,7},{7,6},{8,9},{9,8},{10,11... | collective-permute-start | bytes 3145736 | tf_op jit(solution)/shard_map/ppermute | solution.py:562
  69.6 27.9 %collective-permute-start.2 = (bf16[512,1024]{1,0:T(8,128)(2,1)}, bf16[512,1024]{1,0:T(8,128)(2,1)}, u32[]{:S(2)}, u32[]{:S(2)}) collective-permute-start(bf16[512,1024]{1,0:T(8,128)(2,1)} %get-tuple-element.184.own_ref), channel_id=1, source_target_pairs={{0,1},{1,0},{2,3},{3,2},{4,5},{5,4},{6,7},{7,6},{8,9},{9,8},{10,11... | collective-permute-start | bytes 3145736 | tf_op jit(solution)/shard_map/ppermute | solution.py:562
  98.8 61.6 %collective-permute-start.5 = (bf16[352,1024]{1,0:T(8,128)(2,1)S(1)}, bf16[352,1024]{1,0:T(8,128)(2,1)}, u32[]{:S(2)}, u32[]{:S(2)}) collective-permute-start(bf16[352,1024]{1,0:T(8,128)(2,1)S(1)} %constant_dynamic-slice_fusion.11), channel_id=1, source_target_pairs={{0,1},{1,0},{2,3},{3,2},{4,5},{5,4},{6,7},{7,6},{8,9},{9,8},{10,11... | collective-permute-start | bytes 2162696 | tf_op jit(solution)/shard_map/ppermute | solution.py:562
  102.1 58.2 %collective-permute-start.4 = (bf16[256,1408]{1,0:T(8,128)(2,1)}, bf16[256,1408]{1,0:T(8,128)(2,1)}, u32[]{:S(2)}, u32[]{:S(2)}) collective-permute-start(bf16[256,1408]{1,0:T(8,128)(2,1)} %constant_dynamic-slice_fusion.12), channel_id=1, source_target_pairs={{0,1},{1,0},{2,3},{3,2},{4,5},{5,4},{6,7},{7,6},{8,9},{9,8},{10,11... | collective-permute-start | bytes 2162696 | tf_op jit(solution)/shard_map/ppermute | solution.py:562
  105.3 55.1 %collective-permute-start.3 = (bf16[256,1408]{1,0:T(8,128)(2,1)}, bf16[256,1408]{1,0:T(8,128)(2,1)S(1)}, u32[]{:S(2)}, u32[]{:S(2)}) collective-permute-start(bf16[256,1408]{1,0:T(8,128)(2,1)} %constant_dynamic-slice_fusion.13), channel_id=1, source_target_pairs={{0,1},{1,0},{2,3},{3,2},{4,5},{5,4},{6,7},{7,6},{8,9},{9,8},{10,11... | collective-permute-start | bytes 2162696 | tf_op jit(solution)/shard_map/ppermute | solution.py:562
  159.4 53.6 %collective-permute-start.6 = (bf16[512,1024]{1,0:T(8,128)(2,1)}, bf16[512,1024]{1,0:T(8,128)(2,1)}, u32[]{:S(2)}, u32[]{:S(2)}) collective-permute-start(bf16[512,1024]{1,0:T(8,128)(2,1)} %get-tuple-element.410), channel_id=1, source_target_pairs={{0,1},{1,0},{2,3},{3,2},{4,5},{5,4},{6,7},{7,6},{8,9},{9,8},{10,11... | collective-permute-start | bytes 3145736 | tf_op jit(solution)/shard_map/ppermute | solution.py:562
  160.4 56.3 %collective-permute-start.11 = (bf16[352,1024]{1,0:T(8,128)(2,1)}, bf16[352,1024]{1,0:T(8,128)(2,1)}, u32[]{:S(2)}, u32[]{:S(2)}) collective-permute-start(bf16[352,1024]{1,0:T(8,128)(2,1)} %collective-permute-done.5), channel_id=1, source_target_pairs={{0,4},{2,6},{4,0},{6,2},{8,12},{10,14},{12,8},{14,10},{16,20},{18,... | collective-permute-start | bytes 2162696 | tf_op jit(solution)/shard_map/ppermute | solution.py:568
  161.9 56.3 %collective-permute-start.10 = (bf16[256,1408]{1,0:T(8,128)(2,1)}, bf16[256,1408]{1,0:T(8,128)(2,1)}, u32[]{:S(2)}, u32[]{:S(2)}) collective-permute-start(bf16[256,1408]{1,0:T(8,128)(2,1)} %collective-permute-done.4), channel_id=1, source_target_pairs={{0,4},{2,6},{4,0},{6,2},{8,12},{10,14},{12,8},{14,10},{16,20},{18,... | collective-permute-start | bytes 2162696 | tf_op jit(solution)/shard_map/ppermute | solution.py:568
  162.5 57.4 %collective-permute-start.9 = (bf16[256,1408]{1,0:T(8,128)(2,1)S(1)}, bf16[256,1408]{1,0:T(8,128)(2,1)}, u32[]{:S(2)}, u32[]{:S(2)}) collective-permute-start(bf16[256,1408]{1,0:T(8,128)(2,1)S(1)} %collective-permute-done.3), channel_id=1, source_target_pairs={{0,4},{2,6},{4,0},{6,2},{8,12},{10,14},{12,8},{14,10},{16,20},{18,... | collective-permute-start | bytes 2162696 | tf_op jit(solution)/shard_map/ppermute | solution.py:568
  215.6 21.8 %collective-permute-start.7 = (bf16[512,1024]{1,0:T(8,128)(2,1)S(1)}, bf16[512,1024]{1,0:T(8,128)(2,1)S(1)}, u32[]{:S(2)}, u32[]{:S(2)}) collective-permute-start(bf16[512,1024]{1,0:T(8,128)(2,1)S(1)} %get-tuple-element.412), channel_id=1, source_target_pairs={{0,1},{1,0},{2,3},{3,2},{4,5},{5,4},{6,7},{7,6},{8,9},{9,8},{10,11... | collective-permute-start | bytes 3145736 | tf_op jit(solution)/shard_map/ppermute | solution.py:562
  238.4 10.2 collective-permute-start.14
  239.1 10.8 %collective-permute-start.13 = (bf16[512,1408]{1,0:T(8,128)(2,1)S(1)}, bf16[512,1408]{1,0:T(8,128)(2,1)S(1)}, u32[]{:S(2)}, u32[]{:S(2)}) collective-permute-start(bf16[512,1408]{1,0:T(8,128)(2,1)S(1)} %pad_maximum_fusion.8), channel_id=1, source_target_pairs={{0,2},{2,0},{4,6},{6,4},{8,10},{10,8},{12,14},{14,12},{16,18},{18,... | collective-permute-start | bytes 4325384 | tf_op jit(solution)/shard_map/ppermute | solution.py:565
  244.4 7.4 collective-permute-start.12
  247.8 33.1 %collective-permute-start.8 = (bf16[512,1024]{1,0:T(8,128)(2,1)}, bf16[512,1024]{1,0:T(8,128)(2,1)}, u32[]{:S(2)}, u32[]{:S(2)}) collective-permute-start(bf16[512,1024]{1,0:T(8,128)(2,1)} %get-tuple-element.414), channel_id=1, source_target_pairs={{0,1},{1,0},{2,3},{3,2},{4,5},{5,4},{6,7},{7,6},{8,9},{9,8},{10,11... | collective-permute-start | bytes 3145736 | tf_op jit(solution)/shard_map/ppermute | solution.py:562
  369.6 56.4 %collective-permute-start.18 = (bf16[512,2816]{1,0:T(8,128)(2,1)}, bf16[512,2816]{1,0:T(8,128)(2,1)}, u32[]{:S(2)}, u32[]{:S(2)}) collective-permute-start(bf16[512,2816]{1,0:T(8,128)(2,1)} %constant_dynamic-slice_fusion.7), channel_id=1, source_target_pairs={{0,2},{2,0},{4,6},{6,4},{8,10},{10,8},{12,14},{14,12},{16,18},{18,... | collective-permute-start | bytes 8650760 | tf_op jit(solution)/shard_map/ppermute | solution.py:565
  386.3 44.8 %collective-permute-start.17 = (bf16[512,2816]{1,0:T(8,128)(2,1)}, bf16[512,2816]{1,0:T(8,128)(2,1)}, u32[]{:S(2)}, u32[]{:S(2)}) collective-permute-start(bf16[512,2816]{1,0:T(8,128)(2,1)} %constant_dynamic-slice_fusion.8), channel_id=1, source_target_pairs={{0,2},{2,0},{4,6},{6,4},{8,10},{10,8},{12,14},{14,12},{16,18},{18,... | collective-permute-start | bytes 8650760 | tf_op jit(solution)/shard_map/ppermute | solution.py:565
  399.6 21.1 %collective-permute-start.16 = (bf16[704,1024]{1,0:T(8,128)(2,1)}, bf16[704,1024]{1,0:T(8,128)(2,1)}, u32[]{:S(2)}, u32[]{:S(2)}) collective-permute-start(bf16[704,1024]{1,0:T(8,128)(2,1)} %constant_dynamic-slice_fusion.9), channel_id=1, source_target_pairs={{0,2},{2,0},{4,6},{6,4},{8,10},{10,8},{12,14},{14,12},{16,18},{18,... | collective-permute-start | bytes 4325384 | tf_op jit(solution)/shard_map/ppermute | solution.py:565
  402.9 19.8 %collective-permute-start.15 = (bf16[704,1024]{1,0:T(8,128)(2,1)}, bf16[704,1024]{1,0:T(8,128)(2,1)}, u32[]{:S(2)}, u32[]{:S(2)}) collective-permute-start(bf16[704,1024]{1,0:T(8,128)(2,1)} %constant_dynamic-slice_fusion.10), channel_id=1, source_target_pairs={{0,2},{2,0},{4,6},{6,4},{8,10},{10,8},{12,14},{14,12},{16,18},{18,... | collective-permute-start | bytes 4325384 | tf_op jit(solution)/shard_map/ppermute | solution.py:565
  473.3 98.8 %collective-permute-start.19 = (bf16[1536,1024]{1,0:T(8,128)(2,1)S(1)}, bf16[1536,1024]{1,0:T(8,128)(2,1)S(1)}, u32[]{:S(2)}, u32[]{:S(2)}) collective-permute-start(bf16[1536,1024]{1,0:T(8,128)(2,1)S(1)} %get-tuple-element.267), channel_id=1, source_target_pairs={{0,1},{1,0},{2,3},{3,2},{4,5},{5,4},{6,7},{7,6},{8,9},{9,8},{10,11... | collective-permute-start | bytes 9437192 | tf_op jit(solution)/shard_map/ppermute | solution.py:562
  475.3 20.3 %collective-permute-start.25 = (bf16[352,1024]{1,0:T(8,128)(2,1)S(1)}, bf16[352,1024]{1,0:T(8,128)(2,1)}, u32[]{:S(2)}, u32[]{:S(2)}) collective-permute-start(bf16[352,1024]{1,0:T(8,128)(2,1)S(1)} %constant_dynamic-slice_fusion.3), channel_id=1, source_target_pairs={{0,4},{2,6},{4,0},{6,2},{8,12},{10,14},{12,8},{14,10},{16,20},{18,... | collective-permute-start | bytes 2162696 | tf_op jit(solution)/shard_map/ppermute | solution.py:568
  476.0 49.3 %collective-permute-start.22 = (bf16[256,2816]{1,0:T(8,128)(2,1)S(1)}, bf16[256,2816]{1,0:T(8,128)(2,1)}, u32[]{:S(2)}, u32[]{:S(2)}) collective-permute-start(bf16[256,2816]{1,0:T(8,128)(2,1)S(1)} %constant_dynamic-slice_fusion.5), channel_id=1, source_target_pairs={{0,4},{2,6},{4,0},{6,2},{8,12},{10,14},{12,8},{14,10},{16,20},{18,... | collective-permute-start | bytes 4325384 | tf_op jit(solution)/shard_map/ppermute | solution.py:568
  478.7 77.4 %collective-permute-start.20 = (bf16[256,2816]{1,0:T(8,128)(2,1)}, bf16[256,2816]{1,0:T(8,128)(2,1)S(1)}, u32[]{:S(2)}, u32[]{:S(2)}) collective-permute-start(bf16[256,2816]{1,0:T(8,128)(2,1)} %constant_dynamic-slice_fusion.6), channel_id=1, source_target_pairs={{0,4},{2,6},{4,0},{6,2},{8,12},{10,14},{12,8},{14,10},{16,20},{18,... | collective-permute-start | bytes 4325384 | tf_op jit(solution)/shard_map/ppermute | solution.py:568
  494.0 76.8 %collective-permute-start.24 = (bf16[352,1024]{1,0:T(8,128)(2,1)S(1)}, bf16[352,1024]{1,0:T(8,128)(2,1)S(1)}, u32[]{:S(2)}, u32[]{:S(2)}) collective-permute-start(bf16[352,1024]{1,0:T(8,128)(2,1)S(1)} %constant_dynamic-slice_fusion.4), channel_id=1, source_target_pairs={{0,4},{2,6},{4,0},{6,2},{8,12},{10,14},{12,8},{14,10},{16,20},{18,... | collective-permute-start | bytes 2162696 | tf_op jit(solution)/shard_map/ppermute | solution.py:568
  496.9 73.9 %collective-permute-start.26 = (bf16[352,1024]{1,0:T(8,128)(2,1)S(1)}, bf16[352,1024]{1,0:T(8,128)(2,1)S(1)}, u32[]{:S(2)}, u32[]{:S(2)}) collective-permute-start(bf16[352,1024]{1,0:T(8,128)(2,1)S(1)} %add_convert_fusion.10), channel_id=1, source_target_pairs={{0,1},{1,0},{2,3},{3,2},{4,5},{5,4},{6,7},{7,6},{8,9},{9,8},{10,11... | collective-permute-start | bytes 2162696 | tf_op jit(solution)/shard_map/ppermute | solution.py:562
  527.1 54.4 %collective-permute-start.23 = (bf16[256,1408]{1,0:T(8,128)(2,1)S(1)}, bf16[256,1408]{1,0:T(8,128)(2,1)S(1)}, u32[]{:S(2)}, u32[]{:S(2)}) collective-permute-start(bf16[256,1408]{1,0:T(8,128)(2,1)S(1)} %slice.204), channel_id=1, source_target_pairs={{0,1},{1,0},{2,3},{3,2},{4,5},{5,4},{6,7},{7,6},{8,9},{9,8},{10,11... | collective-permute-start | bytes 2162696 | tf_op jit(solution)/shard_map/ppermute | solution.py:562
  556.5 33.8 %collective-permute-start.21 = (bf16[256,1408]{1,0:T(8,128)(2,1)S(1)}, bf16[256,1408]{1,0:T(8,128)(2,1)S(1)}, u32[]{:S(2)}, u32[]{:S(2)}) collective-permute-start(bf16[256,1408]{1,0:T(8,128)(2,1)S(1)} %slice.202), channel_id=1, source_target_pairs={{0,1},{1,0},{2,3},{3,2},{4,5},{5,4},{6,7},{7,6},{8,9},{9,8},{10,11... | collective-permute-start | bytes 2162696 | tf_op jit(solution)/shard_map/ppermute | solution.py:562
  581.4 9.9 collective-permute-start.27
  591.7 13.7 %collective-permute-start.28 = (bf16[256,1024]{1,0:T(8,128)(2,1)S(1)}, bf16[256,1024]{1,0:T(8,128)(2,1)S(1)}, u32[]{:S(2)}, u32[]{:S(2)}) collective-permute-start(bf16[256,1024]{1,0:T(8,128)(2,1)S(1)} %constant_dynamic-slice_fusion.1), channel_id=1, source_target_pairs={{0,4},{2,6},{4,0},{6,2},{8,12},{10,14},{12,8},{14,10},{16,20},{18,... | collective-permute-start | bytes 1572872 | tf_op jit(solution)/shard_map/ppermute | solution.py:568
  606.4 404.8 %all-reduce.15.cloned.1.call-start = ((), (), s32[]{:S(2)}) async-start(), calls=%async_computation | async-start | bytes 6291456 | tf_op jit(solution)/shard_map/psum | solution.py:594
  793.4 15.2 %collective-permute-start.37 = (bf16[256,1024]{1,0:T(8,128)(2,1)}, bf16[256,1024]{1,0:T(8,128)(2,1)}, u32[]{:S(2)}, u32[]{:S(2)}) collective-permute-start(bf16[256,1024]{1,0:T(8,128)(2,1)} %get-tuple-element.301), channel_id=1, source_target_pairs={{0,4},{2,6},{4,0},{6,2},{8,12},{10,14},{12,8},{14,10},{16,20},{18,... | collective-permute-start | bytes 1572872 | tf_op jit(solution)/shard_map/ppermute | solution.py:568
  795.8 73.5 %collective-permute-start.29 = (bf16[512,3072]{1,0:T(8,128)(2,1)}, bf16[512,3072]{1,0:T(8,128)(2,1)}, u32[]{:S(2)}, u32[]{:S(2)}) collective-permute-start(bf16[512,3072]{1,0:T(8,128)(2,1)} %constant_dynamic-slice_fusion), channel_id=1, source_target_pairs={{0,2},{2,0},{4,6},{6,4},{8,10},{10,8},{12,14},{14,12},{16,18},{18,... | collective-permute-start | bytes 9437192 | tf_op jit(solution)/shard_map/ppermute | solution.py:565
  795.8 28.3 %collective-permute-start.35 = (bf16[352,1024]{1,0:T(8,128)(2,1)}, bf16[352,1024]{1,0:T(8,128)(2,1)}, u32[]{:S(2)}, u32[]{:S(2)}) collective-permute-start(bf16[352,1024]{1,0:T(8,128)(2,1)} %get-tuple-element.300), channel_id=1, source_target_pairs={{0,4},{2,6},{4,0},{6,2},{8,12},{10,14},{12,8},{14,10},{16,20},{18,... | collective-permute-start | bytes 2162696 | tf_op jit(solution)/shard_map/ppermute | solution.py:568
  797.2 42.2 %collective-permute-start.33 = (bf16[256,1408]{1,0:T(8,128)(2,1)S(1)}, bf16[256,1408]{1,0:T(8,128)(2,1)}, u32[]{:S(2)}, u32[]{:S(2)}) collective-permute-start(bf16[256,1408]{1,0:T(8,128)(2,1)S(1)} %copy-done.41), channel_id=1, source_target_pairs={{0,4},{2,6},{4,0},{6,2},{8,12},{10,14},{12,8},{14,10},{16,20},{18,... | collective-permute-start | bytes 2162696 | tf_op jit(solution)/shard_map/ppermute | solution.py:568
  797.8 55.0 %collective-permute-start.31 = (bf16[256,1408]{1,0:T(8,128)(2,1)S(1)}, bf16[256,1408]{1,0:T(8,128)(2,1)}, u32[]{:S(2)}, u32[]{:S(2)}) collective-permute-start(bf16[256,1408]{1,0:T(8,128)(2,1)S(1)} %copy-done.40), channel_id=1, source_target_pairs={{0,4},{2,6},{4,0},{6,2},{8,12},{10,14},{12,8},{14,10},{16,20},{18,... | collective-permute-start | bytes 2162696 | tf_op jit(solution)/shard_map/ppermute | solution.py:568
  808.6 69.5 %collective-permute-start.30 = (bf16[1536,1024]{1,0:T(8,128)(2,1)}, bf16[1536,1024]{1,0:T(8,128)(2,1)}, u32[]{:S(2)}, u32[]{:S(2)}) collective-permute-start(bf16[1536,1024]{1,0:T(8,128)(2,1)} %get-tuple-element.297), channel_id=1, source_target_pairs={{0,1},{1,0},{2,3},{3,2},{4,5},{5,4},{6,7},{7,6},{8,9},{9,8},{10,11... | collective-permute-start | bytes 9437192 | tf_op jit(solution)/shard_map/ppermute | solution.py:562
  824.0 30.1 %collective-permute-start.38 = (bf16[512,1024]{1,0:T(8,128)(2,1)S(1)}, bf16[512,1024]{1,0:T(8,128)(2,1)S(1)}, u32[]{:S(2)}, u32[]{:S(2)}) collective-permute-start(bf16[512,1024]{1,0:T(8,128)(2,1)S(1)} %pad_maximum_fusion.13), channel_id=1, source_target_pairs={{0,2},{2,0},{4,6},{6,4},{8,10},{10,8},{12,14},{14,12},{16,18},{18,... | collective-permute-start | bytes 3145736 | tf_op jit(solution)/shard_map/ppermute | solution.py:565
  839.5 18.3 %collective-permute-start.36 = (bf16[704,1024]{1,0:T(8,128)(2,1)S(1)}, bf16[704,1024]{1,0:T(8,128)(2,1)S(1)}, u32[]{:S(2)}, u32[]{:S(2)}) collective-permute-start(bf16[704,1024]{1,0:T(8,128)(2,1)S(1)} %pad_maximum_fusion.12), channel_id=1, source_target_pairs={{0,2},{2,0},{4,6},{6,4},{8,10},{10,8},{12,14},{14,12},{16,18},{18,... | collective-permute-start | bytes 4325384 | tf_op jit(solution)/shard_map/ppermute | solution.py:565
  852.8 9.1 collective-permute-start.34
  854.2 11.2 %collective-permute-start.32 = (bf16[512,1408]{1,0:T(8,128)(2,1)S(1)}, bf16[512,1408]{1,0:T(8,128)(2,1)S(1)}, u32[]{:S(2)}, u32[]{:S(2)}) collective-permute-start(bf16[512,1408]{1,0:T(8,128)(2,1)S(1)} %pad_maximum_fusion.10), channel_id=1, source_target_pairs={{0,2},{2,0},{4,6},{6,4},{8,10},{10,8},{12,14},{14,12},{16,18},{18,... | collective-permute-start | bytes 4325384 | tf_op jit(solution)/shard_map/ppermute | solution.py:565
  900.1 1.4 collective-permute-start.39
  901.5 4.9 collective-permute-start.40
  906.4 13.1 %collective-permute-start.41 = (f32[19,1024]{1,0:T(8,128)S(1)}, f32[19,1024]{1,0:T(8,128)S(1)}, u32[]{:S(2)}, u32[]{:S(2)}) collective-permute-start(f32[19,1024]{1,0:T(8,128)S(1)} %add.324), channel_id=1, source_target_pairs={{0,8},{2,10},{4,12},{6,14},{8,0},{10,2},{12,4},{14,6},{16,24},{18,... | collective-permute-start | bytes 233480 | tf_op jit(solution)/shard_map/ppermute | solution.py:602
  919.5 10.2 collective-permute-start.42
  929.8 3.8 collective-permute-start.43
  1011.3 5.9 collective-permute-start.44
  (92 other events, 844.5 us)
Sparse Core Ops, SparseCore 0:
  606.5 107.7 all-reduce.16
  878.3 132.9 all-reduce.14
